TPU v7x, 32 devices: a whole 2x2x4 slice. The times are simulated.
32 devices in a mesh: row: 8 (over z, core), col: 4 (over y, x).
Axes of the slice: x: 2, y: 2, z: 4, core: 2. Of those that a mesh axis runs over, the one named last changes fastest.
Arguments:
- latents: bfloat16 [128, 512, 256], P('row', 'col'), may hold values from -64 to 64
- code_ids: int32 [128, 512], P('row', 'col'), may hold values from 0 to 16383, as said below
- norm_gain: float32 [256], replicated, may hold values from 0.1 to 1.9
- norm_bias: float32 [256], replicated, may hold values from -2 to 2
- encoder_weight: bfloat16 [3, 3, 256, 256], replicated, may hold values from -0.125 to 0.125
- codebook: bfloat16 [16384, 256], replicated, may hold values from -6 to 6
- decoder_weight: bfloat16 [3, 3, 256, 256], replicated, may hold values from -0.125 to 0.125
- decoded_cotangent: bfloat16 [128, 512, 256], P('row', 'col'), may hold values from -6 to 6
Outputs:
- decoded: bfloat16 [128, 512, 256], P('row', 'col')
- latents_grad: bfloat16 [128, 512, 256], P('row', 'col')
- norm_gain_grad: float32 [256], replicated
- norm_bias_grad: float32 [256], replicated
- encoder_weight_grad: float32 [3, 3, 256, 256], replicated
- decoder_weight_grad: float32 [3, 3, 256, 256], replicated
- codebook_grad: float32 [16384, 256], P(('row', 'col'))
Inputs may be any that keep to these rules, and one draw needn't show every extreme that they name: On the 16 x 128 positions of one device, at most 128 code_ids fall in any one aligned block of 512 codes; in every draw one block holds exactly 128 of them on every device.
All inputs are finite; a program needn't handle non-finite values.
Results may differ from a plain program's by a relative error of at most 0.002.
The roundings to bfloat16 on the way count: a program that leaves them out, or rounds other values in their place, can miss the bound.
Values may be sent and summed in bfloat16 or wider, within the bound.
No kernel may reach another device: no remote copies, remote signals or barrier semaphores. Data moves between devices by JAX's collectives and lax.ppermute only.
A program may use at most 128 MiB of HBM per device.

v0:
```python
import jax
import jax.numpy as jnp
from jax import lax
from jax.experimental import pallas as pl
from jax.experimental.pallas import tpu as pltpu
from jax.sharding import PartitionSpec as P

G = 32
epsilon = 1e-06
commit_beta = 0.25
F32 = jnp.float32
BF16 = jnp.bfloat16
F16 = jnp.float16
AXES = ("row", "col")
SIDE = 8
HALO = 2
VMEM = pl.BlockSpec(memory_space=pltpu.VMEM)
SMEM = pl.BlockSpec(memory_space=pltpu.SMEM)
ANY = pl.BlockSpec(memory_space=pltpu.HBM)
NT = (((1,), (1,)), ((), ()))
NN = (((1,), (0,)), ((), ()))
HIGH = lax.Precision.HIGHEST


class Late:
    def __init__(self, ref, copy):
        self.ref, self.copy = ref, copy
        copy.start()

    def get(self):
        if self.copy is not None:
            self.copy.wait()
            self.copy = None
        return self.ref


def call(kernel, ins, outs, scratch=(), specs=None, flops=0, moved=0, room=16, late=(), far=()):
    room = 56 if late else room
    specs = list(specs or [VMEM] * len(ins))
    first = len(ins) + len(jax.tree.leaves(outs)) + len(scratch)
    scratch = list(scratch)
    for i, field in late:
        specs[i] = ANY
        shape = ins[i].shape if field is None else ins[i].shape[1:]
        scratch.append(pltpu.VMEM(shape, ins[i].dtype))
    if late:
        scratch.append(pltpu.SemaphoreType.DMA((len(late),)))

    def wrapped(*refs):
        given = list(refs[:first])
        loads = []
        for j, (i, field) in enumerate(late):
            source = refs[i] if field is None else refs[i].at[field]
            copy = pltpu.make_async_copy(source, refs[first + j], refs[-1].at[j])
            given[i] = Late(refs[first + j], copy)
            loads.append(given[i])
        kernel(*given)
        for load in loads:
            load.get()

    return pl.pallas_call(
        wrapped,
        in_specs=specs,
        out_specs=jax.tree.unflatten(
            jax.tree.structure(outs),
            [ANY if i in far else VMEM for i in range(len(jax.tree.leaves(outs)))],
        ),
        out_shape=outs,
        scratch_shapes=scratch,
        compiler_params=pltpu.CompilerParams(vmem_limit_bytes=room * 2**20),
        cost_estimate=pl.CostEstimate(flops=flops, bytes_accessed=moved, transcendentals=0),
    )(*ins)


def use(*refs):
    return [ref.get() if isinstance(ref, Late) else ref for ref in refs]


def shaped(shape, dtype=F32):
    return jax.ShapeDtypeStruct(shape, dtype)


def dot(a, b, dims=NN, precision=None):
    return lax.dot_general(a, b, dims, precision=precision, preferred_element_type=F32)


def front_kernel(devices, shard, cap, lat, ids, payload, slots):
    height, width = ids.shape
    count = height * width

    owner = lax.broadcasted_iota(jnp.int32, (devices, width), 0)
    upper = (
        lax.broadcasted_iota(jnp.int32, (width, width), 0)
        < lax.broadcasted_iota(jnp.int32, (width, width), 1)
    ).astype(BF16)
    slot_row = lax.broadcasted_iota(jnp.int32, (width, width), 0)
    members, codes, dests = [], [], []
    for r in range(height):
        code = ids[r : r + 1, :]
        dest = code // shard
        codes.append(code - dest * shard)
        dests.append(dest)
        members.append((owner == dest).astype(F32))
    stacked = jnp.concatenate([x.astype(BF16) for x in members], 0)
    before = dot(stacked, upper)
    base = jnp.zeros((devices, 1), F32)
    hits, parts = [], []
    for r in range(height):
        member = members[r]
        count_before = before[r * devices : (r + 1) * devices] + base
        rank = jnp.sum(member * count_before, 0, keepdims=True).astype(jnp.int32)
        slots[r : r + 1, :] = dests[r] * cap + rank
        hits.append((slot_row == rank).astype(BF16))
        tagged = codes[r] + 1
        high = tagged // 32
        low = tagged - high * 32
        both = [member * high.astype(F32), member * low.astype(F32)]
        parts.append(jnp.concatenate(both, 0).astype(BF16))
        base = base + jnp.sum(member, 1, keepdims=True)
    placed = dot(jnp.concatenate(parts, 1), jnp.concatenate(hits, 1), NT)
    placed = 32.0 * placed[:devices] + placed[devices:]
    (lat,) = use(lat)
    channels = lat.shape[2]

    def add_row(r, total):
        return total + jnp.sum(lat[r].astype(F32), 0, keepdims=True)

    mean = lax.fori_loop(0, height, add_row, jnp.zeros((1, channels), F32)) * (1.0 / count)

    def add_square(r, total):
        gap = lat[r].astype(F32) - mean
        return total + jnp.sum(gap * gap, 0, keepdims=True)

    square = lax.fori_loop(0, height, add_square, jnp.zeros((1, channels), F32))
    half = width
    rows = [mean[:, :half], mean[:, half:], square[:, :half], square[:, half:]]
    for i, part in enumerate(rows):
        payload[:, i, :] = jnp.broadcast_to(part, (devices, half))
    payload[:, 4, :] = placed
    payload[:, 5:, :] = jnp.zeros((devices, 3, half), F32)


def place_of():
    return (
        lax.axis_index("row"),
        lax.axis_index("col"),
        lax.axis_size("row"),
        lax.axis_size("col"),
    )


def place_of():
    return (
        lax.axis_index("row"),
        lax.axis_index("col"),
        lax.axis_size("row"),
        lax.axis_size("col"),
    )


def fill_tile(scr, own, left, right, up, down, ring):
    height, width, channels = own.shape
    pitch = width + 2 * SIDE
    for r in range(height):
        base = SIDE + (ring + r) * pitch
        scr[base + SIDE - HALO : base + SIDE] = left[r].astype(F32)
        scr[base + SIDE : base + SIDE + width] = own[r].astype(F32)
        scr[base + SIDE + width : base + SIDE + width + HALO] = right[r].astype(F32)
    span = up.shape[1]
    for i in range(ring):
        top = SIDE + i * pitch + SIDE - HALO
        scr[top : top + span] = up[HALO - ring + i].astype(F32)
        low = SIDE + (ring + height + i) * pitch + SIDE - HALO
        scr[low : low + span] = down[i].astype(F32)
    blank = jnp.zeros((SIDE - HALO, channels), F32)
    for r in range(height + 2 * ring):
        base = SIDE + r * pitch
        scr[base : base + SIDE - HALO] = blank
        scr[base + pitch - SIDE + HALO : base + pitch] = blank
    ends(scr, channels)


def ends(scr, channels):
    blank = jnp.zeros((SIDE, channels), F32)
    scr[0:SIDE] = blank
    scr[scr.shape[0] - SIDE :] = blank


def spread(scr, wide, count, pitch, channels):
    def one(r, _):
        value = scr[pl.ds(pl.multiple_of(r * pitch, 8), pitch + 2 * SIDE), :]
        at = pl.ds(pl.multiple_of(r * pitch, 16), pitch)
        for j in range(3):
            start = SIDE + j - 1
            wide[at, j * channels : (j + 1) * channels] = value[start : start + pitch].astype(BF16)
        return 0

    lax.fori_loop(0, count, one, 0)


def rows_at(r, pitch, count):
    if isinstance(r, int):
        return slice(r * pitch, (r + count) * pitch)
    return pl.ds(pl.multiple_of(r * pitch, 16), count * pitch)


def forward_rows(wide, weight, r, step, pitch):
    total = dot(wide[rows_at(r, pitch, step), :], weight[0])
    for dy in (1, 2):
        total = total + dot(wide[rows_at(r + dy, pitch, step), :], weight[dy])
    return total


def backward_rows(wide, weight, r, step, pitch):
    total = dot(wide[rows_at(r + 2, pitch, step), :], weight[0], NT)
    for dy in (1, 2):
        total = total + dot(wide[rows_at(r + 2 - dy, pitch, step), :], weight[dy], NT)
    return total


def kernel_grad(turned, wide, keep, give, pitch, height, first_row):
    channels = turned.shape[0]
    half = channels // 2
    count = height * pitch
    core = lax.axis_index("row") % 2
    for dy in range(3):
        start = (first_row + 1 - dy) * pitch
        product = dot(turned[...], wide[start : start + count, :])
        for j in range(3):
            at = (dy * 3 + 2 - j) * channels
            low = product[:, j * channels : j * channels + half]
            high = product[:, j * channels + half : (j + 1) * channels]

            keep[at : at + channels, :] = jnp.where(core == 0, low, high)
            give[at : at + channels, :] = jnp.where(core == 0, high, low)


def turn_own(own, turned):
    height, width, channels = own.shape
    pitch = width + 2 * SIDE
    blank = jnp.zeros((SIDE, channels), F32)
    for r in range(0, height, 8):
        parts = []
        for k in range(8):
            parts += [blank, own[r + k].astype(F32), blank]
        block = jnp.concatenate(parts, 0)
        turned[:, r * pitch : (r + 8) * pitch] = block.T.astype(BF16)


def decoder_grad_kernel(
    cot, codes, left, right, up, down, keep, give, scr, wide, turned
):
    cot, left, right, up, down = use(cot, left, right, up, down)
    height, width, channels = cot.shape
    pitch = width + 2 * SIDE
    fill_tile(scr, cot, left, right, up, down, 1)
    spread(scr, wide, height + 2, pitch, channels)
    turn_own(*use(codes), turned)
    kernel_grad(turned, wide, keep, give, pitch, height, 1)


def decoder_kernel(codes, left, right, up, down, weight, out, scr, wide):
    codes, left, right, up, down = use(codes, left, right, up, down)
    height, width, channels = codes.shape
    pitch = width + 2 * SIDE
    fill_tile(scr, codes, left, right, up, down, 1)
    spread(scr, wide, height + 2, pitch, channels)
    step = 4
    (weight,) = use(weight)

    def part(k, _):
        value = forward_rows(wide, weight, k * step, step, pitch)
        for u in range(step):
            at = u * pitch + SIDE
            out[k * step + u] = value[at : at + width].astype(BF16)
        return 0

    lax.fori_loop(0, height // step, part, 0)


def group_stats(gathered, height, width):
    devices = gathered.shape[0]
    rows, cols = lax.axis_size("row"), lax.axis_size("col")
    local = jnp.concatenate([gathered[:, 0, :], gathered[:, 1, :]], 1)
    square = jnp.concatenate([gathered[:, 2, :], gathered[:, 3, :]], 1)
    channels = local.shape[1]
    per_group = channels // G
    same = lax.broadcasted_iota(jnp.int32, (channels, channels), 0) // per_group
    same = same == lax.broadcasted_iota(jnp.int32, (channels, channels), 1) // per_group
    mix = jnp.where(same, 1.0 / per_group, 0.0).astype(F32)
    centre = jnp.broadcast_to(jnp.sum(local, 0, keepdims=True) * (1.0 / devices), (8, channels))
    mean = dot(centre, mix, precision=HIGH)[0:1]
    gap = local - mean
    spread_sum = square + (height * width) * (gap * gap)
    total = jnp.sum(spread_sum, 0, keepdims=True) * (1.0 / (devices * height * width))
    var = dot(jnp.broadcast_to(total, (8, channels)), mix, precision=HIGH)[0:1]
    return mean, lax.rsqrt(var + epsilon)


def inside_tile(row, col, rows, cols, height, width):
    pitch = width + 2 * SIDE
    place = lax.broadcasted_iota(jnp.int32, (pitch + 2 * SIDE, 1), 0) - 2 * SIDE + col * width
    inside_col = (place >= 0) & (place < cols * width)

    def keep(line):
        high = row * height + line
        return inside_col & (high >= 0) & (high < rows * height)

    return keep


def encoder_kernel(
    code_scale,
    lat, left, right, up, down, codes, gathered, gain, bias, weight,
    z_far, pull, turned_far, stats, power,
    tmp_s, wide, z_out, turned, own_s, sems,
):
    height, width, channels = codes.ref.shape
    pitch = width + 2 * SIDE
    keep = inside_tile(*place_of(), height, width)
    mean, inv = group_stats(gathered, height, width)
    stats[0:1, :] = mean
    stats[1:2, :] = inv
    fill_tile(tmp_s, *use(lat, left, right, up, down), 2)
    scale = inv * gain[...]
    offset = bias[...]

    blank = jnp.zeros((SIDE, channels), F32)

    def smooth_row(r):
        act = (tmp_s[r * pitch : (r + 1) * pitch + 2 * SIDE, :] - mean) * scale + offset
        value = jnp.where(keep(r - 2), act * jax.nn.sigmoid(act), 0.0)
        at = slice(r * pitch, (r + 1) * pitch)
        for j in range(3):
            start = SIDE + j - 1
            wide[at, j * channels : (j + 1) * channels] = value[start : start + pitch].astype(BF16)
        if 2 <= r < height + 2:
            base = (r - 2) * pitch
            own_s[base : base + SIDE, :] = blank
            own_s[base + SIDE : base + SIDE + width, :] = value[2 * SIDE : 2 * SIDE + width]
            own_s[base + SIDE + width : base + pitch, :] = blank

    step = 3
    steps = (height + 2) // step
    ends(z_out, channels)
    weight, codes = use(weight, codes)

    def z_copy(k):
        at = slice(SIDE + k * step * pitch, SIDE + (k + 1) * step * pitch)
        return pltpu.make_async_copy(z_out.at[at, :], z_far.at[at, :], sems.at[k])

    def part(k):
        first = SIDE + k * step * pitch
        count = step * pitch
        z = tmp_s[first + pitch : first + pitch + count, :]
        z = z + forward_rows(wide, weight, k * step, step, pitch)
        z_out[first : first + count, :] = z
        z_copy(k).start()
        tops = []
        for u in range(step):
            line = k * step + u - 1
            if 0 <= line < height:
                at = u * pitch + SIDE
                some = (codes[line].astype(F32) - z[at : at + width]) * code_scale
                pull[line * width : (line + 1) * width, :] = some
                tops.append(jnp.max(jnp.abs(some), 0, keepdims=True))
        return tops

    for r in range(step + 2):
        smooth_row(r)
    tops = []
    for k in range(steps):
        for r in range((k + 1) * step + 2, min((k + 2) * step + 2, height + 4)):
            smooth_row(r)
        tops += part(k)
    for r in range(0, height, 8):
        at = slice(r * pitch, (r + 8) * pitch)
        turned[:, at] = own_s[at, :].T.astype(BF16)
    turned_copy = pltpu.make_async_copy(turned, turned_far, sems.at[steps])
    turned_copy.start()
    top = jnp.max(jnp.concatenate(tops, 0), 0, keepdims=True)
    top = jnp.max(top, 1, keepdims=True)
    power[...] = jnp.broadcast_to(exponent(top), power.shape)
    for k in range(steps):
        z_copy(k).wait()
    turned_copy.wait()


def pack_kernel(slots, pull, power, packed):
    packed[...] = jnp.zeros(packed.shape, F32)
    scale = jnp.exp2(power[0:1, :])

    def some(i, _):
        value = pull[pl.ds(pl.multiple_of(i * 16, 8), 16), :] * scale
        for u in range(16):
            packed[pl.ds(slots[i * 16 + u], 1), :] = value[u : u + 1, :]
        return 0

    lax.fori_loop(0, pull.shape[0] // 16, some, 0)


def flip_weight(weight, flipped):
    channels = weight.shape[2]
    for dy in range(3):
        for j in range(3):
            flipped[dy, :, j * channels : (j + 1) * channels] = weight[dy, 2 - j]


def rotate_kernel(
    cot, left, right, up, down, codes, code_l, code_r, code_u, code_d, z_in, turned, dec_w, power,
    plane_far, keep_grad, give_grad,
    tmp_s, code_s, wide, back_wide, flipped, plane, sem,
):
    height, width, channels = cot.ref.shape
    pitch = width + 2 * SIDE
    fill_tile(tmp_s, *use(cot, left, right, up, down), 2)
    spread(tmp_s, wide, height + 4, pitch, channels)
    fill_tile(code_s, *use(codes, code_l, code_r, code_u, code_d), 1)
    flip_weight(*use(dec_w), flipped)
    ends(plane, channels)
    step = 3
    chunks = (height + 2) // step

    def part(k):
        at = slice(SIDE + k * step * pitch, SIDE + (k + 1) * step * pitch)
        plane[at, :] = backward_rows(wide, flipped, k * step, step, pitch)

    block = 24
    z_in, turned = use(z_in, turned)
    place = lax.broadcasted_iota(jnp.int32, (block, 1), 0)
    row, col, rows, cols = place_of()

    def total(x):
        return jnp.sum(x, 1, keepdims=True)

    def turn(line):
        spots = [
            slice(SIDE + line * pitch + b, SIDE + line * pitch + b + block)
            for b in range(0, pitch, block)
        ]
        sums = []
        for at in spots:
            z, e = z_in[at, :], code_s[at, :]
            sums.append((total(z * z) + epsilon, total(e * e) + epsilon))
        scales = []
        for at, (zz, ee) in zip(spots, sums):
            z, e, back = z_in[at, :], code_s[at, :], plane[at, :]
            z_inv, e_inv = lax.rsqrt(zz), lax.rsqrt(ee)
            e_unit = e * e_inv
            mirror = z * z_inv + e_unit
            scales.append(
                (z_inv, e_inv, ee, total(mirror * mirror) + epsilon, total(mirror * back),
                 total(e_unit * back))
            )
        high = row * height + line - 1
        keep = (high >= 0) & (high < rows * height)
        for b, (at, (z_inv, e_inv, ee, mm, along, code)) in enumerate(zip(spots, scales)):
            z, e, back = z_in[at, :], code_s[at, :], plane[at, :]
            stretch = ee * e_inv * z_inv
            along = 2.0 * along / mm
            z_part = stretch * z_inv * (2.0 * code - along) + commit_beta
            e_part = stretch * e_inv * along + commit_beta
            across = place + b * block - SIDE + col * width
            inside = keep & (across >= 0) & (across < cols * width)
            plane[at, :] = jnp.where(inside, stretch * back + z_part * z - e_part * e, 0.0)

    part(0)
    for k in range(chunks):
        if k + 1 < chunks:
            part(k + 1)
        for u in range(step):
            turn(k * step + u)
    plane_copy = pltpu.make_async_copy(plane, plane_far, sem)
    plane_copy.start()
    spread(plane, back_wide, height + 2, pitch, channels)
    kernel_grad(turned, back_wide, keep_grad, give_grad, pitch, height, 1)
    taps, half = keep_grad.shape[0] - 8, keep_grad.shape[1]
    lane = lax.broadcasted_iota(jnp.int32, (8, half), 1)
    mine = jnp.where(lane == row * cols + col, power[:, :half], 0.0)
    keep_grad[taps:, :] = mine
    give_grad[taps:, :] = mine
    plane_copy.wait()


def back_kernel(lat, plane, stats, gain, bias, enc_w, back_act, tail, back_wide, flipped):
    (plane,) = use(plane)
    height, width, channels = lat.ref.shape
    pitch = width + 2 * SIDE
    spread(plane, back_wide, height + 2, pitch, channels)
    flip_weight(*use(enc_w), flipped)
    (lat,) = use(lat)
    mean, inv = stats[0:1, :], stats[1:2, :]
    step = 4

    def last(k, totals):
        value = backward_rows(back_wide, flipped, k * step, step, pitch)
        first, second = totals
        for u in range(step):
            at = u * pitch + SIDE
            normed = (lat[k * step + u].astype(F32) - mean) * inv
            act = normed * gain[...] + bias[...]
            s = jax.nn.sigmoid(act)
            some = value[at : at + width] * s * (1.0 + act * (1.0 - s))
            back_act[k * step + u] = some
            first = first + jnp.sum(some, 0, keepdims=True)
            second = second + jnp.sum(some * normed, 0, keepdims=True)
        return first, second

    zero = jnp.zeros((1, channels), F32)
    first, second = lax.fori_loop(0, height // step, last, (zero, zero))
    half = channels // 2
    lines = [first[:, :half], first[:, half:], second[:, :half], second[:, half:]]
    tail[...] = jnp.concatenate(lines + [jnp.zeros((4, half), F32)], 0)


def last_kernel(lat, back_act, plane, stats, gain, *refs):
    pieces, (out, grads) = refs[:-2], refs[-2:]
    height, width, channels = lat.shape
    mean, inv = stats[0:1, :], stats[1:2, :]
    per_group = channels // G
    count = height * width * lax.axis_size("row") * lax.axis_size("col") * per_group
    end = pieces[0].shape[1] - 24
    sums = jnp.zeros((8, pieces[0].shape[2]), F32)
    for ref in pieces:
        for z in range(ref.shape[0]):
            some = ref[z, end : end + 8, :] + ref[z, end + 8 : end + 16, :]
            sums = sums + some * jnp.exp2(-ref[z, end + 18 : end + 19, :])
    first = jnp.concatenate([sums[0:1, :], sums[1:2, :]], 1)
    second = jnp.concatenate([sums[2:3, :], sums[3:4, :]], 1)
    grads[0:1, :] = first
    grads[1:2, :] = second
    same = lax.broadcasted_iota(jnp.int32, (channels, channels), 0) // per_group
    same = same == lax.broadcasted_iota(jnp.int32, (channels, channels), 1) // per_group
    mix = jnp.where(same, 1.0, 0.0).astype(F32)
    both = jnp.concatenate([first * gain[...], second * gain[...]] + [first] * 6, 0)
    means = dot(both, mix, precision=HIGH) * (1.0 / count)

    lat, back_act, plane = use(lat, back_act, plane)

    def one(r, _):
        normed = (lat[r].astype(F32) - mean) * inv
        d = back_act[r] * gain[...]
        at = pl.multiple_of((r + 1) * (width + 2 * SIDE) + 2 * SIDE, 8)
        enc_back = plane[pl.ds(at, width), :]
        out[r] = (inv * (d - means[0:1] - normed * means[1:2]) + enc_back).astype(BF16)
        return 0

    lax.fori_loop(0, height, one, 0)


def owner_kernel(tags, wide, out):
    shard, channels = out.shape
    total = jnp.zeros((shard, 2 * channels), F32)
    rows = wide.shape[0]
    chunk = 1024
    code = lax.broadcasted_iota(jnp.int32, (shard, tags.shape[1]), 0) + 1
    lines = chunk // tags.shape[1]
    for k in range(rows // chunk):
        hit = jnp.concatenate(
            [
                (code == tags[k * lines + u : k * lines + u + 1, :]).astype(F32).astype(BF16)
                for u in range(lines)
            ],
            1,
        )
        total = total + dot(hit, wide[k * chunk : (k + 1) * chunk, :])
    out[...] = total[:, :channels] + total[:, channels:]


def exponent(biggest):
    return 14.0 - jnp.ceil(jnp.log2(jnp.maximum(biggest, 1e-30)))


def exchange(x):
    return lax.all_to_all(x, AXES, split_axis=0, concat_axis=0, tiled=True)


def pair_swap(x):
    size = lax.axis_size("row")
    return lax.ppermute(x, "row", [(i, i ^ 1) for i in range(size)])


def shifts(n, stride=1):
    size = n * stride
    return [[((i + s * stride) % size, i) for i in range(size)] for s in range(1, n)]


def columns_kernel(cols, *refs):
    ins, outs = refs[:-cols], refs[-cols:]
    col = lax.axis_index("col")
    extra = ins[0].shape[0] % 256
    taps = ins[0].shape[0] - extra
    lines = taps // cols
    for s, out in enumerate(outs):
        at = pl.ds(pl.multiple_of((col + cols - s) % cols * lines, 8), lines)
        out[:lines, :] = ins[0][at, :] + ins[1][at, :]
        if extra:
            out[lines:, :] = ins[0][taps:, :] + ins[1][taps:, :]


def rows_kernel(cols, *refs):
    parts, outs = (refs[:cols], refs[cols : 2 * cols]), refs[2 * cols :]
    row, _, rows, _ = place_of()
    depth = rows // 2
    lines = outs[0].shape[0] // 2 - 4

    def added(some, first, count):
        value = some[0][first : first + count, :]
        for ref in some[1:]:
            value = value + ref[first : first + count, :]
        return value

    tail = added(parts[0], depth * lines, 8)
    tops = [jnp.zeros((1, tail.shape[1]), F32)] * 2
    for z in range(depth):
        values = [added(some, z * lines, lines) for some in parts]
        tops = [
            jnp.maximum(top, jnp.max(jnp.abs(some), 0, keepdims=True))
            for top, some in zip(tops, values)
        ]
        for s, out in enumerate(outs):

            @pl.when((row // 2 + depth - s) % depth == z)
            def _():
                for i in range(2):
                    out[i * lines : (i + 1) * lines, :] = values[i]

    end = 2 * lines
    powers = [exponent(jnp.max(top, 1, keepdims=True)) for top in tops]
    outs[0][end:, :] = tail
    for out in outs[1:]:
        out[end : end + 8, :] = tail
        out[end + 8 :, :] = jnp.zeros((8, tail.shape[1]), F32)
        for i, power in enumerate(powers):
            at = slice(i * lines, (i + 1) * lines)
            out[at, :] = out[at, :] * jnp.exp2(power)
            out[end + 8 + i : end + 9 + i, :] = jnp.broadcast_to(power, (1, tail.shape[1]))


def chunk_kernel(depth, *refs):
    parts, (tail, tail_b, out, powers) = refs[:depth], refs[depth:]
    half = out.shape[1]
    lines = parts[0].shape[0] // 2 - 4
    end = 2 * lines
    total = parts[0][end:, :]
    values = [parts[0][i * lines : (i + 1) * lines, :] for i in range(2)]
    for ref in parts[1:]:
        total = total + ref[end : end + 8, :]
        for i in range(2):
            scale = jnp.exp2(-ref[end + 8 + i : end + 9 + i, :])
            values[i] = values[i] + ref[i * lines : (i + 1) * lines, :] * scale
    powers[...] = total
    values.append(tail[...] + tail_b[...])
    end = 2 * lines + 16
    out[end:, :] = jnp.zeros((8, half), F32)
    for i, some in enumerate(values):
        top = jnp.max(jnp.max(jnp.abs(some), 0, keepdims=True), 1, keepdims=True)
        power = exponent(top)
        some = some * jnp.exp2(power)
        if i < 2:
            out[i * lines : (i + 1) * lines, :] = some
        else:
            high = some.astype(BF16).astype(F32)
            out[end - 16 : end - 8, :] = high
            out[end - 8 : end, :] = some - high
        out[end + i : end + i + 1, :] = jnp.broadcast_to(power, (1, half))


def column_parts(arrays):
    cols = lax.axis_size("col")
    taps, half = arrays[0].shape
    extra = taps % 256
    parts = call(
        lambda *refs: columns_kernel(cols, *refs),
        arrays,
        [shaped(((taps - extra) // cols + extra, half))] * cols,
        moved=4 * 10**6,
    )
    return list(parts)


def column_send(parts):
    cols = lax.axis_size("col")
    return [parts[0]] + [lax.ppermute(x, "col", p) for x, p in zip(parts[1:], shifts(cols))]


def row_sums(enc, dec, tail):
    cols, depth = len(enc), lax.axis_size("row") // 2
    taps, half = dec[0].shape
    lines = taps // depth
    parts = call(
        lambda *refs: rows_kernel(cols, *refs),
        enc + dec,
        [shaped((2 * lines + 8, half))] + [shaped((2 * lines + 16, half))] * (depth - 1),
        moved=4 * 10**6,
    )
    sent = [x.astype(F16) for x in parts[1:]]
    sent = [lax.ppermute(x, "row", p) for x, p in zip(sent, shifts(depth, 2))]
    parts = [parts[0]] + [x.astype(F32) for x in sent]
    return call(
        lambda *refs: chunk_kernel(depth, *refs),
        parts + [tail, pair_swap(tail)],
        (shaped((2 * lines + 24, half)), shaped((8, half))),
        moved=10**6,
    )


def gather_rows(chunk):
    own = chunk.astype(F16)
    steps = shifts(lax.axis_size("row") // 2, 2)
    return jnp.stack([own] + [lax.ppermute(own, "row", p) for p in steps])


def gather_columns(own):
    return [own] + [lax.ppermute(own, "col", p) for p in shifts(lax.axis_size("col"))]


def gather_cores(own, other):
    rows, cols = lax.axis_size("row"), lax.axis_size("col")
    lines, half = own[0].shape[1] // 2 - 12, own[0].shape[2]
    chunks = cols * rows // 2
    return call(
        lambda *refs: assemble_kernel(lines, *refs),
        own + other,
        (shaped((chunks, lines, 2 * half)), shaped((chunks, lines, 2 * half))),
        moved=10**7,
    )


def assemble_kernel(lines, *refs):
    pieces, outs = refs[:-2], refs[-2:]
    row, col, rows, cols = place_of()
    depth = rows // 2
    half = outs[0].shape[2] // 2
    for k, ref in enumerate(pieces):
        core = (row + k // cols) % 2
        c = (col + k % cols) % cols
        lanes = pl.ds(pl.multiple_of(core * half, half), half)
        for s in range(depth):
            z = (row // 2 + s) % depth
            for i, out in enumerate(outs):
                at = 2 * lines + 16 + i
                scale = jnp.exp2(-ref[s, at : at + 1, :])
                value = ref[s, i * lines : (i + 1) * lines, :] * scale
                out[c * depth + z, :, lanes] = value


def halo(fields):
    rows, cols = lax.axis_size("row"), lax.axis_size("col")
    forth = lambda n: [(i, i + 1) for i in range(n - 1)]
    back = lambda n: [(i + 1, i) for i in range(n - 1)]
    left_edge = jnp.stack([x[:, :HALO] for x in fields])
    right_edge = jnp.stack([x[:, -HALO:] for x in fields])
    left = lax.ppermute(right_edge, "col", forth(cols))
    right = lax.ppermute(left_edge, "col", back(cols))

    def lines(at):
        return jnp.concatenate([left[:, at], jnp.stack([x[at] for x in fields]), right[:, at]], 2)

    up = lax.ppermute(lines(slice(-HALO, None)), "row", forth(rows))
    down = lax.ppermute(lines(slice(0, HALO)), "row", back(rows))
    return left, right, up, down


def body(
    latents,
    code_ids,
    norm_gain,
    norm_bias,
    encoder_weight,
    codebook,
    decoder_weight,
    decoded_cotangent,
):
    height, width, channels = latents.shape
    devices = lax.axis_size("row") * lax.axis_size("col")
    codes_total = codebook.shape[0]
    shard = codes_total // devices
    count = height * width
    cap = 2 * count // devices
    pitch = width + 2 * SIDE
    conv_flops = 2 * count * 9 * channels * channels
    taps = 9 * channels
    half = channels // 2
    plane = (height + 2) * pitch
    plane_rows = plane + 2 * SIDE
    big = (height + 4) * pitch
    after = lambda *x: lax.optimization_barrier(x)
    halos = lambda field, start: [(start + i, field) for i in range(4)]

    payload, slots = call(
        lambda *refs: front_kernel(devices, shard, cap, *refs),
        (latents, code_ids),
        (shaped((devices, 8, width)), shaped((height, width), jnp.int32)),
        flops=10**9,
        moved=10**6,
        late=[(0, None)],
    )
    payload, code_ids, latents, decoded_cotangent = after(
        payload, code_ids, latents, decoded_cotangent
    )
    gathered = exchange(payload)
    quantized = codebook[code_ids]
    left, right, up, down = halo((latents, decoded_cotangent, quantized))
    gain = norm_gain.reshape(1, channels)
    bias = norm_bias.reshape(1, channels)

    dec_grad = call(
        decoder_grad_kernel,
        (decoded_cotangent, quantized, left, right, up, down),
        (shaped((taps, half)), shaped((taps, half))),
        [
            pltpu.VMEM((plane_rows, channels), F32),
            pltpu.VMEM((plane, 3 * channels), BF16),
            pltpu.VMEM((channels, height * pitch), BF16),
        ],
        flops=conv_flops,
        moved=5 * 10**6,
        late=[(0, None), *halos(1, 2), (1, None)],
    )
    dec_keep, dec_give = dec_grad
    gathered, dec_keep, dec_give = after(gathered, dec_keep, dec_give)
    dec_parts = column_parts((dec_keep, pair_swap(dec_give)))
    gathered, *dec_parts = after(gathered, *dec_parts)
    dec_parts = column_send(dec_parts)
    enc_fwd = encoder_weight.reshape(3, 3 * channels, channels)
    dec_fwd = decoder_weight.reshape(3, 3 * channels, channels)
    code_scale = codes_total / (count * devices)
    z, pull, turned, stats, power = call(
        lambda *refs: encoder_kernel(code_scale, *refs),
        (latents, left, right, up, down, quantized, gathered, gain, bias, enc_fwd),
        (
            shaped((plane_rows, channels)),
            shaped((count, channels)),
            shaped((channels, height * pitch), BF16),
            shaped((8, channels)),
            shaped((8, channels)),
        ),
        [
            pltpu.VMEM((big + 2 * SIDE, channels), F32),
            pltpu.VMEM((big, 3 * channels), BF16),
            pltpu.VMEM((plane_rows, channels), F32),
            pltpu.VMEM((channels, height * pitch), BF16),
            pltpu.VMEM((height * pitch, channels), F32),
            pltpu.SemaphoreType.DMA(((height + 2) // 3 + 1,)),
        ],
        far=(0, 2),
        flops=conv_flops,
        moved=10 * 10**6,
        room=20,
        late=[(0, None), *halos(0, 1), (9, None), (5, None)],
    )
    packed = call(
        pack_kernel,
        (slots.reshape(-1), pull, power),
        shaped((devices * cap, channels)),
        specs=[SMEM, VMEM, VMEM],
        flops=5 * 10**9,
        moved=6 * 10**6,
    )
    send = packed.astype(F16).reshape(devices, cap, channels)
    send, z, *dec_parts = after(send, z, *dec_parts)
    received = exchange(send)

    back_plane, keep_grad, give_grad = call(
        rotate_kernel,
        (
            decoded_cotangent, left, right, up, down, quantized, left, right, up, down, z, turned,
            decoder_weight, power,
        ),
        (
            shaped((plane_rows, channels)),
            shaped((taps + 8, half)),
            shaped((taps + 8, half)),
        ),
        [
            pltpu.VMEM((big + 2 * SIDE, channels), F32),
            pltpu.VMEM((plane_rows, channels), F32),
            pltpu.VMEM((big, 3 * channels), BF16),
            pltpu.VMEM((plane, 3 * channels), BF16),
            pltpu.VMEM((3, channels, 3 * channels), BF16),
            pltpu.VMEM((plane_rows, channels), F32),
            pltpu.SemaphoreType.DMA,
        ],
        far=(0,),
        flops=2 * conv_flops,
        moved=15 * 10**6,
        room=32,
        late=[
            (0, None), *halos(1, 1), (5, None), *halos(2, 6), (12, None), (10, None), (11, None)
        ],
    )
    enc_parts = column_send(column_parts((keep_grad, pair_swap(give_grad))))
    back_act, tail = call(
        back_kernel,
        (latents, back_plane, stats, gain, bias, encoder_weight),
        (shaped((height, width, channels)), shaped((8, half))),
        [
            pltpu.VMEM((plane, 3 * channels), BF16),
            pltpu.VMEM((3, channels, 3 * channels), BF16),
        ],
        flops=conv_flops,
        moved=8 * 10**6,
        late=[(1, None), (5, None), (0, None)],
    )
    decoded = call(
        decoder_kernel,
        (quantized, left, right, up, down, dec_fwd),
        shaped((height, width, channels), BF16),
        [
            pltpu.VMEM((plane_rows, channels), F32),
            pltpu.VMEM((plane, 3 * channels), BF16),
        ],
        flops=conv_flops,
        moved=4 * 10**6,
        late=[(0, None), *halos(2, 1), (5, None)],
    )
    decoded, *enc_parts = after(decoded, *enc_parts)
    chunk, powers = row_sums(enc_parts, dec_parts, tail)
    own = gather_rows(chunk)
    pieces = gather_columns(own)

    rows_f = received.astype(F32) * jnp.exp2(-jnp.round(powers[0, :devices]))[:, None, None]
    rows_f = rows_f.reshape(devices * cap, channels)
    high = lax.reduce_precision(rows_f, 8, 7)
    low = rows_f - high
    wide = jnp.concatenate([high.astype(BF16), low.astype(BF16)], 1)
    tags = gathered[:, 4, :cap].astype(jnp.int32).reshape(-1, 128)
    codebook_grad = call(
        owner_kernel,
        (tags, wide),
        shaped((shard, channels)),
        flops=2 * 10**9,
        moved=6 * 10**6,
    )
    codebook_grad, *pieces = after(codebook_grad, *pieces)
    other = [pair_swap(x) for x in pieces]
    own = [x.astype(F32) for x in pieces]
    latents_grad, norm_grads = call(
        last_kernel,
        (latents, back_act, back_plane, stats, gain, *own),
        (shaped((height, width, channels), BF16), shaped((2, channels))),
        flops=10**8,
        moved=6 * 10**6,
    )
    other = [x.astype(F32) for x in other]
    encoder_weight_grad, decoder_weight_grad = [
        x.reshape(3, 3, channels, channels) for x in gather_cores(own, other)
    ]
    return (
        decoded,
        latents_grad,
        norm_grads[1],
        norm_grads[0],
        encoder_weight_grad,
        decoder_weight_grad,
        codebook_grad,
    )


def solution(mesh):
    return jax.shard_map(
        body,
        mesh=mesh,
        in_specs=(
            P("row", "col", None),
            P("row", "col"),
            P(),
            P(),
            P(),
            P(),
            P(),
            P("row", "col", None),
        ),
        out_specs=(
            P("row", "col", None),
            P("row", "col", None),
            P(),
            P(),
            P(),
            P(),
            P(("row", "col"), None),
        ),
        check_vma=False,
    )
```

profile of v0, /device:TPU:0, one launch (start us, length us, event | category | flops | bytes accessed | tf_op | source)
XLA Modules:
  0.0 169.1 jit_solution(13588707457429091834)
XLA Ops:
  0.6 3.6 %shard_map.135 = (f32[32,8,128]{2,1,0:T(8,128)}, s32[16,128]{1,0:T(8,128)}) custom-call(bf16[16,128,256]{2,1,0:T(8,128)(2,1)} %refs_0_.6, s32[16,128]{1,0:T(8,128)} %refs_1_.1), custom_call_target="tpu_custom_call" | custom-call | flops 1000000000 | bytes 1000000 | tf_op jit(solution)/shard_map/pallas_call | solution.py:61
  4.3 11.1 %gather_fusion = bf16[2048,256]{1,0:T(8,128)(2,1)S(1)} fusion(bf16[16384,256]{1,0:T(8,128)(2,1)} %param.13, s32[2048]{0:T(1024)S(1)} %fusion.3), kind=kCustom, calls=%fused_computation | custom fusion | bytes 2105344 | tf_op jit(solution)/shard_map/gather | solution.py:803
  15.4 1.3 slice_bitcast_fusion.6
  16.8 4.8 %collective-permute-start = (bf16[3,16,2,256]{3,2,1,0:T(2,128)(2,1)S(1)}, bf16[3,16,2,256]{3,2,1,0:T(2,128)(2,1)S(1)}, u32[]{:S(2)}, u32[]{:S(2)}) collective-permute-start(bf16[3,16,2,256]{3,2,1,0:T(2,128)(2,1)S(1)} %pad_maximum_fusion.4), channel_id=1, source_target_pairs={{0,1},{1,2},{2,3},{4,5},{5,6},{6,7},{8,9},{9,10},{10,11},{12,13},{... | collective-permute-start | bytes 147464 | tf_op jit(solution)/shard_map/ppermute | solution.py:754
  21.8 1.3 collective-permute-start.1
  23.1 1.1 slice_bitcast_fusion
  24.2 3.5 %collective-permute-done.1.refs_2_.refs_3_.refs_7_ = bf16[3,16,2,256]{3,2,1,0:T(2,128)(2,1)S(1)} collective-permute-done((bf16[3,16,2,256]{3,2,1,0:T(2,128)(2,1)S(1)}, bf16[3,16,2,256]{3,2,1,0:T(2,128)(2,1)S(1)}, u32[]{:S(2)}, u32[]{:S(2)}) %collective-permute-start.1) | collective-permute-done | bytes 49184 | tf_op jit(solution)/shard_map/ppermute | solution.py:755
  27.8 0.1 pad_maximum_fusion.1
  27.9 1.3 collective-permute-start.2
  29.3 0.1 pad_maximum_fusion.2
  29.4 1.3 collective-permute-start.3
  30.7 8.8 %all-to-all-start = ((f32[32,8,128]{2,1,0:T(8,128)}), f32[32,8,128]{2,1,0:T(8,128)S(1)}, u32[]{:S(2)}, u32[]{:S(2)}) async-start(f32[32,8,128]{2,1,0:T(8,128)} %get-tuple-element.72), calls=%async_computation | async-start | bytes 262144 | tf_op jit(solution)/shard_map/all_to_all | solution.py:575
  39.5 0.7 copy-done.17
  40.2 0.8 copy-done.18
  41.0 6.8 %shard_map.137 = (f32[2304,128]{1,0:T(8,128)}, f32[2304,128]{1,0:T(8,128)}) custom-call(bf16[16,128,256]{2,1,0:T(8,128)(2,1)} %refs_0_.4, bf16[16,128,256]{2,1,0:T(8,128)(2,1)} %bitcast.54, bf16[3,16,2,256]{3,2,1,0:T(2,128)(2,1)} %copy-done.15, bf16[3,16,2,256]{3,2,1,0:T(2,128)(2,1)} %copy-done.16, bf16[3,2,132,256]{3,2,1,0:T(8,128)(2,1)} %copy-done.17, ...), custom_call_target="tpu_custom_call" | custom-call | flops 2415919104 | bytes 5000000 | tf_op jit(solution)/shard_map/pallas_call | solution.py:61
  47.7 0.1 all-to-all-done.refs_6_
  47.8 0.8 collective-permute-start.4
  48.7 2.7 %collective-permute-done.4.refs_1_ = f32[2304,128]{1,0:T(8,128)S(1)} collective-permute-done((f32[2304,128]{1,0:T(8,128)}, f32[2304,128]{1,0:T(8,128)S(1)}, u32[]{:S(2)}, u32[]{:S(2)}) %collective-permute-start.4) | collective-permute-done | bytes 1179680 | tf_op jit(solution)/shard_map/ppermute | solution.py:580
  51.4 1.3 copy-done.4
  52.6 0.1 shard_map.138
  52.7 2.3 %collective-permute-start.5 = (f32[576,128]{1,0:T(8,128)S(1)}, f32[576,128]{1,0:T(8,128)S(1)}, u32[]{:S(2)}, u32[]{:S(2)}) collective-permute-start(f32[576,128]{1,0:T(8,128)S(1)} %get-tuple-element.87), channel_id=1, source_target_pairs={{1,0},{2,1},{3,2},{0,3},{5,4},{6,5},{7,6},{4,7},{9,8},{10,9},{11,1... | collective-permute-start | bytes 884744 | tf_op jit(solution)/shard_map/ppermute | solution.py:684
  55.0 2.0 %collective-permute-start.6 = (f32[576,128]{1,0:T(8,128)S(1)}, f32[576,128]{1,0:T(8,128)S(1)}, u32[]{:S(2)}, u32[]{:S(2)}) collective-permute-start(f32[576,128]{1,0:T(8,128)S(1)} %get-tuple-element.88), channel_id=1, source_target_pairs={{2,0},{3,1},{0,2},{1,3},{6,4},{7,5},{4,6},{5,7},{10,8},{11,9},{8,1... | collective-permute-start | bytes 884744 | tf_op jit(solution)/shard_map/ppermute | solution.py:684
  57.0 9.9 %shard_map.139 = (f32[2608,256]{1,0:T(8,128)}, f32[2048,256]{1,0:T(8,128)}, bf16[256,2304]{1,0:T(8,128)(2,1)}, f32[8,256]{1,0:T(8,128)}, f32[8,256]{1,0:T(8,128)}) custom-call(bf16[16,128,256]{2,1,0:T(8,128)(2,1)} %refs_0_.6, bf16[3,16,2,256]{3,2,1,0:T(2,128)(2,1)} %copy-done.15, bf16[3,16,2,256]{3,2,1,0:T(2,128)(2,1)} %copy-done.16, ...), custom_call_target="tpu_custom_call" | custom-call | flops 2415919104 | bytes 10000000 | tf_op jit(solution)/shard_map/pallas_call | solution.py:61
  66.9 1.6 copy-done.9
  68.5 0.7 copy-done.10
  69.2 5.3 %shard_map.140 = f32[4096,256]{1,0:T(8,128)S(1)} custom-call(s32[2048]{0:T(1024)S(1)} %bitcast.52, f32[2048,256]{1,0:T(8,128)S(1)} %copy-done.9, f32[8,256]{1,0:T(8,128)S(1)} %copy-done.10), custom_call_target="tpu_custom_call" | custom-call | flops 5000000000 | bytes 6000000 | tf_op jit(solution)/shard_map/pallas_call | solution.py:61
  74.5 1.6 convert_element_type.62
  76.2 5.3 %all-to-all-start.1 = ((f16[32,128,256]{2,1,0:T(8,128)(2,1)}), f16[32,128,256]{2,1,0:T(8,128)(2,1)S(1)}, u32[]{:S(2)}, u32[]{:S(2)}) async-start(f16[32,128,256]{2,1,0:T(8,128)(2,1)} %bitcast.19), calls=%async_computation.1 | async-start | bytes 4194304 | tf_op jit(solution)/shard_map/all_to_all | solution.py:575
  81.5 13.9 %shard_map.141 = (f32[2608,256]{1,0:T(8,128)}, f32[2312,128]{1,0:T(8,128)}, f32[2312,128]{1,0:T(8,128)}) custom-call(bf16[16,128,256]{2,1,0:T(8,128)(2,1)} %refs_0_.4, bf16[3,16,2,256]{3,2,1,0:T(2,128)(2,1)} %copy-done.15, bf16[3,16,2,256]{3,2,1,0:T(2,128)(2,1)} %copy-done.16, bf16[3,2,132,256]{3,2,1,0:T(8,128)(2,1)} %copy-done.17, ...), custom_call_target="tpu_custom_call" | custom-call | flops 4831838208 | bytes 15000000 | tf_op jit(solution)/shard_map/pallas_call | solution.py:61
  95.5 0.3 collective-permute-start.8
  95.8 2.8 %collective-permute-done.8.refs_1_ = f32[2312,128]{1,0:T(8,128)S(1)} collective-permute-done((f32[2312,128]{1,0:T(8,128)}, f32[2312,128]{1,0:T(8,128)S(1)}, u32[]{:S(2)}, u32[]{:S(2)}) %collective-permute-start.8) | collective-permute-done | bytes 1183776 | tf_op jit(solution)/shard_map/ppermute | solution.py:580
  98.6 1.3 copy-done.3
  99.9 0.1 shard_map.142
  100.0 2.7 %collective-permute-start.9 = (f32[584,128]{1,0:T(8,128)S(1)}, f32[584,128]{1,0:T(8,128)S(1)}, u32[]{:S(2)}, u32[]{:S(2)}) collective-permute-start(f32[584,128]{1,0:T(8,128)S(1)} %get-tuple-element.95), channel_id=1, source_target_pairs={{1,0},{2,1},{3,2},{0,3},{5,4},{6,5},{7,6},{4,7},{9,8},{10,9},{11,1... | collective-permute-start | bytes 897032 | tf_op jit(solution)/shard_map/ppermute | solution.py:684
  102.7 0.6 collective-permute-start.10
  103.3 0.6 collective-permute-start.11
  103.9 6.7 %shard_map.136 = bf16[16,128,256]{2,1,0:T(8,128)(2,1)} custom-call(bf16[16,128,256]{2,1,0:T(8,128)(2,1)} %bitcast.57, bf16[3,16,2,256]{3,2,1,0:T(2,128)(2,1)} %copy-done.15, bf16[3,16,2,256]{3,2,1,0:T(2,128)(2,1)} %copy-done.16, bf16[3,2,132,256]{3,2,1,0:T(8,128)(2,1)} %copy-done.17, bf16[3,2,132,256]{3,2,1,0:T(8,128)(2,1)} %copy-done.18, ...), custom_call_target="tpu_custom_call" | custom-call | flops 2415919104 | bytes 4000000 | tf_op jit(solution)/shard_map/pallas_call | solution.py:61
  110.6 8.5 %shard_map.143 = (f32[16,128,256]{2,1,0:T(8,128)}, f32[8,128]{1,0:T(8,128)}) custom-call(bf16[16,128,256]{2,1,0:T(8,128)(2,1)} %refs_0_.6, f32[2608,256]{1,0:T(8,128)} %get-tuple-element.99.refs_1_.refs_2_, f32[8,256]{1,0:T(8,128)} %get-tuple-element.100.refs_2_.refs_3_, f32[1,256]{1,0:T(1,128)} %bitcast.50, f32[1,256]{1,0:T(1,128)} %bitcast.70, ...), custom_call_target="tpu_custom_call" | custom-call | flops 2415919104 | bytes 8000000 | tf_op jit(solution)/shard_map/pallas_call | solution.py:61
  119.3 5.0 %collective-permute-done.10.refs_2_ = f32[584,128]{1,0:T(8,128)S(1)} collective-permute-done((f32[584,128]{1,0:T(8,128)S(1)}, f32[584,128]{1,0:T(8,128)S(1)}, u32[]{:S(2)}, u32[]{:S(2)}) %collective-permute-start.10) | collective-permute-done | bytes 299040 | tf_op jit(solution)/shard_map/ppermute | solution.py:684
  124.2 0.4 shard_map.144
  124.6 3.0 %collective-permute-start.12 = (f16[304,128]{1,0:T(8,128)(2,1)S(1)}, f16[304,128]{1,0:T(8,128)(2,1)S(1)}, u32[]{:S(2)}, u32[]{:S(2)}) collective-permute-start(f16[304,128]{1,0:T(8,128)(2,1)S(1)} %convert_element_type.66), channel_id=1, source_target_pairs={{8,0},{12,4},{16,8},{20,12},{24,16},{28,20},{0,24},{4,28},{9,1},{1... | collective-permute-start | bytes 233480 | tf_op jit(solution)/shard_map/ppermute | solution.py:698
  127.6 2.2 %collective-permute-start.13 = (f16[304,128]{1,0:T(8,128)(2,1)S(1)}, f16[304,128]{1,0:T(8,128)(2,1)S(1)}, u32[]{:S(2)}, u32[]{:S(2)}) collective-permute-start(f16[304,128]{1,0:T(8,128)(2,1)S(1)} %convert_element_type.68), channel_id=1, source_target_pairs={{16,0},{20,4},{24,8},{28,12},{0,16},{4,20},{8,24},{12,28},{17,1},{... | collective-permute-start | bytes 233480 | tf_op jit(solution)/shard_map/ppermute | solution.py:698
  129.8 2.1 %collective-permute-start.14 = (f16[304,128]{1,0:T(8,128)(2,1)S(1)}, f16[304,128]{1,0:T(8,128)(2,1)S(1)}, u32[]{:S(2)}, u32[]{:S(2)}) collective-permute-start(f16[304,128]{1,0:T(8,128)(2,1)S(1)} %convert_element_type.70), channel_id=1, source_target_pairs={{24,0},{28,4},{0,8},{4,12},{8,16},{12,20},{16,24},{20,28},{25,1},{... | collective-permute-start | bytes 233480 | tf_op jit(solution)/shard_map/ppermute | solution.py:698
  131.9 5.0 %collective-permute-done.13 = f16[304,128]{1,0:T(8,128)(2,1)S(1)} collective-permute-done((f16[304,128]{1,0:T(8,128)(2,1)S(1)}, f16[304,128]{1,0:T(8,128)(2,1)S(1)}, u32[]{:S(2)}, u32[]{:S(2)}) %collective-permute-start.13) | collective-permute-done | bytes 77856 | tf_op jit(solution)/shard_map/ppermute | solution.py:698
  137.0 0.2 shard_map.145
  137.2 1.6 collective-permute-start.17
  138.9 2.3 %collective-permute-start.16 = (f16[312,128]{1,0:T(8,128)(2,1)S(1)}, f16[312,128]{1,0:T(8,128)(2,1)S(1)}, u32[]{:S(2)}, u32[]{:S(2)}) collective-permute-start(f16[312,128]{1,0:T(8,128)(2,1)S(1)} %convert_element_type.74), channel_id=1, source_target_pairs={{8,0},{12,4},{16,8},{20,12},{24,16},{28,20},{0,24},{4,28},{9,1},{1... | collective-permute-start | bytes 239624 | tf_op jit(solution)/shard_map/ppermute | solution.py:711
  141.1 2.4 %collective-permute-done.18 = f16[312,128]{1,0:T(8,128)(2,1)S(1)} collective-permute-done((f16[312,128]{1,0:T(8,128)(2,1)S(1)}, f16[312,128]{1,0:T(8,128)(2,1)S(1)}, u32[]{:S(2)}, u32[]{:S(2)}) %collective-permute-start.18) | collective-permute-done | bytes 79904 | tf_op jit(solution)/shard_map/ppermute | solution.py:711
  143.6 1.2 collective-permute-done.17
  144.7 0.1 pad_maximum_fusion.3
  144.9 4.1 %collective-permute-start.19 = (f16[4,312,128]{2,1,0:T(8,128)(2,1)S(1)}, f16[4,312,128]{2,1,0:T(8,128)(2,1)S(1)}, u32[]{:S(2)}, u32[]{:S(2)}) collective-permute-start(f16[4,312,128]{2,1,0:T(8,128)(2,1)S(1)} %pad_maximum_fusion.3), channel_id=1, source_target_pairs={{1,0},{2,1},{3,2},{0,3},{5,4},{6,5},{7,6},{4,7},{9,8},{10,9},{11,1... | collective-permute-start | bytes 958472 | tf_op jit(solution)/shard_map/ppermute | solution.py:715
  149.0 0.5 collective-permute-start.20
  149.5 0.6 collective-permute-start.21
  150.1 0.6 convert_multiply_fusion
  150.7 0.9 reduce-precision_convert_fusion
  151.6 0.3 pad_maximum_fusion.refs_1_
  152.0 3.1 %shard_map.146 = f32[512,256]{1,0:T(8,128)} custom-call(s32[32,128]{1,0:T(8,128)S(1)} %fusion.1.refs_0_, bf16[4096,512]{1,0:T(8,128)(2,1)S(1)} %pad_maximum_fusion.refs_1_), custom_call_target="tpu_custom_call" | custom-call | flops 2000000000 | bytes 6000000 | tf_op jit(solution)/shard_map/pallas_call | solution.py:61
  155.1 1.7 %collective-permute-done.19 = f16[4,312,128]{2,1,0:T(8,128)(2,1)S(1)} collective-permute-done((f16[4,312,128]{2,1,0:T(8,128)(2,1)S(1)}, f16[4,312,128]{2,1,0:T(8,128)(2,1)S(1)}, u32[]{:S(2)}, u32[]{:S(2)}) %collective-permute-start.19) | collective-permute-done | bytes 319520 | tf_op jit(solution)/shard_map/ppermute | solution.py:715
  156.8 5.6 %collective-permute-done.20 = f16[4,312,128]{2,1,0:T(8,128)(2,1)S(1)} collective-permute-done((f16[4,312,128]{2,1,0:T(8,128)(2,1)S(1)}, f16[4,312,128]{2,1,0:T(8,128)(2,1)S(1)}, u32[]{:S(2)}, u32[]{:S(2)}) %collective-permute-start.20) | collective-permute-done | bytes 319520 | tf_op jit(solution)/shard_map/ppermute | solution.py:715
  162.4 0.5 collective-permute-start.23
  162.9 0.5 collective-permute-start.25
  163.7 2.0 %shard_map.147 = (bf16[16,128,256]{2,1,0:T(8,128)(2,1)}, f32[2,256]{1,0:T(2,128)S(1)}) custom-call(bf16[16,128,256]{2,1,0:T(8,128)(2,1)S(1)} %copy-done.2, f32[16,128,256]{2,1,0:T(8,128)S(1)} %copy-done.1, f32[2608,256]{1,0:T(8,128)S(1)} %copy-done, f32[8,256]{1,0:T(8,128)S(1)} %copy-done.5, f32[1,256]{1,0:T(1,128)S(1)} %bitcast.51, ...), custom_call_target="tpu_custom_call" | custom-call | flops 100000000 | bytes 6000000 | tf_op jit(solution)/shard_map/pallas_call | solution.py:61
  165.7 0.6 fusion.7
  166.5 2.6 %shard_map.148 = (f32[16,144,256]{2,1,0:T(8,128)}, f32[16,144,256]{2,1,0:T(8,128)}) custom-call(f32[4,312,128]{2,1,0:T(8,128)S(1)} %convert_element_type.75.refs_5_.refs_0_, f32[4,312,128]{2,1,0:T(8,128)S(1)} %convert_element_type.76.refs_6_.refs_1_, f32[4,312,128]{2,1,0:T(8,128)S(1)} %convert_element_type.77.refs_7_.refs_2_, ...), custom_call_target="tpu_custom_call" | custom-call | bytes 10000000 | tf_op jit(solution)/shard_map/pallas_call | solution.py:61
  (81 shorter events, 1.0 us)
Async XLA Ops:
  0.6 3.6 %copy-start.14 = (s32[16,128]{1,0:T(8,128)S(1)}, s32[16,128]{1,0:T(8,128)}, u32[]{:S(2)}) copy-start(s32[16,128]{1,0:T(8,128)} %refs_1_.1) | copy-start | bytes 24580
  15.4 24.1 %copy-start.11 = (bf16[2048,256]{1,0:T(8,128)(2,1)}, bf16[2048,256]{1,0:T(8,128)(2,1)S(1)}, u32[]{:S(2)}) copy-start(bf16[2048,256]{1,0:T(8,128)(2,1)S(1)} %gather_fusion) | copy-start | bytes 3145732
  16.8 10.9 %collective-permute-start = (bf16[3,16,2,256]{3,2,1,0:T(2,128)(2,1)S(1)}, bf16[3,16,2,256]{3,2,1,0:T(2,128)(2,1)S(1)}, u32[]{:S(2)}, u32[]{:S(2)}) collective-permute-start(bf16[3,16,2,256]{3,2,1,0:T(2,128)(2,1)S(1)} %pad_maximum_fusion.4), channel_id=1, source_target_pairs={{0,1},{1,2},{2,3},{4,5},{5,6},{6,7},{8,9},{9,10},{10,11},{12,13},{... | collective-permute-start | bytes 147464 | tf_op jit(solution)/shard_map/ppermute | solution.py:754
  21.8 6.0 %collective-permute-start.1 = (bf16[3,16,2,256]{3,2,1,0:T(2,128)(2,1)S(1)}, bf16[3,16,2,256]{3,2,1,0:T(2,128)(2,1)S(1)}, u32[]{:S(2)}, u32[]{:S(2)}) collective-permute-start(bf16[3,16,2,256]{3,2,1,0:T(2,128)(2,1)S(1)} %pad_maximum_fusion.5), channel_id=1, source_target_pairs={{1,0},{2,1},{3,2},{5,4},{6,5},{7,6},{9,8},{10,9},{11,10},{13,12},{... | collective-permute-start | bytes 147464 | tf_op jit(solution)/shard_map/ppermute | solution.py:755
  27.8 11.7 %copy-start.16 = (bf16[3,16,2,256]{3,2,1,0:T(2,128)(2,1)}, bf16[3,16,2,256]{3,2,1,0:T(2,128)(2,1)S(1)}, u32[]{:S(2)}) copy-start(bf16[3,16,2,256]{3,2,1,0:T(2,128)(2,1)S(1)} %collective-permute-done.1.refs_2_.refs_3_.refs_7_) | copy-start | bytes 147460
  27.8 11.7 %copy-start.15 = (bf16[3,16,2,256]{3,2,1,0:T(2,128)(2,1)}, bf16[3,16,2,256]{3,2,1,0:T(2,128)(2,1)S(1)}, u32[]{:S(2)}) copy-start(bf16[3,16,2,256]{3,2,1,0:T(2,128)(2,1)S(1)} %collective-permute-done.refs_1_.refs_2_.refs_6_) | copy-start | bytes 147460
  27.9 11.5 %collective-permute-start.2 = (bf16[3,2,132,256]{3,2,1,0:T(8,128)(2,1)S(1)}, bf16[3,2,132,256]{3,2,1,0:T(8,128)(2,1)S(1)}, u32[]{:S(2)}, u32[]{:S(2)}) collective-permute-start(bf16[3,2,132,256]{3,2,1,0:T(8,128)(2,1)S(1)} %pad_maximum_fusion.1), channel_id=1, source_target_pairs={{0,4},{4,8},{8,12},{12,16},{16,20},{20,24},{24,28},{1,5},{5,9},{9,... | collective-permute-start | bytes 1216520 | tf_op jit(solution)/shard_map/ppermute | solution.py:760
  29.4 10.1 %collective-permute-start.3 = (bf16[3,2,132,256]{3,2,1,0:T(8,128)(2,1)S(1)}, bf16[3,2,132,256]{3,2,1,0:T(8,128)(2,1)S(1)}, u32[]{:S(2)}, u32[]{:S(2)}) collective-permute-start(bf16[3,2,132,256]{3,2,1,0:T(8,128)(2,1)S(1)} %pad_maximum_fusion.2), channel_id=1, source_target_pairs={{4,0},{8,4},{12,8},{16,12},{20,16},{24,20},{28,24},{5,1},{9,5},{13... | collective-permute-start | bytes 1216520 | tf_op jit(solution)/shard_map/ppermute | solution.py:761
  30.7 17.2 %all-to-all-start = ((f32[32,8,128]{2,1,0:T(8,128)}), f32[32,8,128]{2,1,0:T(8,128)S(1)}, u32[]{:S(2)}, u32[]{:S(2)}) async-start(f32[32,8,128]{2,1,0:T(8,128)} %get-tuple-element.72), calls=%async_computation | async-start | bytes 262144 | tf_op jit(solution)/shard_map/all_to_all | solution.py:575
  39.4 0.8 copy-start.17
  40.2 0.8 copy-start.18
  47.8 9.1 %copy-start.12 = (f32[32,8,128]{2,1,0:T(8,128)}, f32[32,8,128]{2,1,0:T(8,128)S(1)}, u32[]{:S(2)}) copy-start(f32[32,8,128]{2,1,0:T(8,128)S(1)} %all-to-all-done.refs_6_) | copy-start | bytes 393220
  47.8 3.5 %collective-permute-start.4 = (f32[2304,128]{1,0:T(8,128)}, f32[2304,128]{1,0:T(8,128)S(1)}, u32[]{:S(2)}, u32[]{:S(2)}) collective-permute-start(f32[2304,128]{1,0:T(8,128)} %get-tuple-element.77), channel_id=1, source_target_pairs={{0,4},{4,0},{8,12},{12,8},{16,20},{20,16},{24,28},{28,24},{1,5},{5... | collective-permute-start | bytes 3538952 | tf_op jit(solution)/shard_map/ppermute | solution.py:580
  51.4 1.3 copy-start.4
  52.7 23.4 %collective-permute-start.5 = (f32[576,128]{1,0:T(8,128)S(1)}, f32[576,128]{1,0:T(8,128)S(1)}, u32[]{:S(2)}, u32[]{:S(2)}) collective-permute-start(f32[576,128]{1,0:T(8,128)S(1)} %get-tuple-element.87), channel_id=1, source_target_pairs={{1,0},{2,1},{3,2},{0,3},{5,4},{6,5},{7,6},{4,7},{9,8},{10,9},{11,1... | collective-permute-start | bytes 884744 | tf_op jit(solution)/shard_map/ppermute | solution.py:684
  55.0 21.2 %collective-permute-start.6 = (f32[576,128]{1,0:T(8,128)S(1)}, f32[576,128]{1,0:T(8,128)S(1)}, u32[]{:S(2)}, u32[]{:S(2)}) collective-permute-start(f32[576,128]{1,0:T(8,128)S(1)} %get-tuple-element.88), channel_id=1, source_target_pairs={{2,0},{3,1},{0,2},{1,3},{6,4},{7,5},{4,6},{5,7},{10,8},{11,9},{8,1... | collective-permute-start | bytes 884744 | tf_op jit(solution)/shard_map/ppermute | solution.py:684
  57.0 19.2 %collective-permute-start.7 = (f32[576,128]{1,0:T(8,128)S(1)}, f32[576,128]{1,0:T(8,128)S(1)}, u32[]{:S(2)}, u32[]{:S(2)}) collective-permute-start(f32[576,128]{1,0:T(8,128)S(1)} %get-tuple-element.89), channel_id=1, source_target_pairs={{3,0},{0,1},{1,2},{2,3},{7,4},{4,5},{5,6},{6,7},{11,8},{8,9},{9,10... | collective-permute-start | bytes 884744 | tf_op jit(solution)/shard_map/ppermute | solution.py:684
  57.0 10.0 %copy-start.8 = (s32[16,128]{1,0:T(8,128)S(1)}, s32[16,128]{1,0:T(8,128)}, u32[]{:S(2)}) copy-start(s32[16,128]{1,0:T(8,128)} %get-tuple-element.71) | copy-start | bytes 24580
  66.9 1.6 copy-start.9
  68.5 0.7 copy-start.10
  76.2 73.9 %all-to-all-start.1 = ((f16[32,128,256]{2,1,0:T(8,128)(2,1)}), f16[32,128,256]{2,1,0:T(8,128)(2,1)S(1)}, u32[]{:S(2)}, u32[]{:S(2)}) async-start(f16[32,128,256]{2,1,0:T(8,128)(2,1)} %bitcast.19), calls=%async_computation.1 | async-start | bytes 4194304 | tf_op jit(solution)/shard_map/all_to_all | solution.py:575
  95.5 3.1 %collective-permute-start.8 = (f32[2312,128]{1,0:T(8,128)}, f32[2312,128]{1,0:T(8,128)S(1)}, u32[]{:S(2)}, u32[]{:S(2)}) collective-permute-start(f32[2312,128]{1,0:T(8,128)} %get-tuple-element.93), channel_id=1, source_target_pairs={{0,4},{4,0},{8,12},{12,8},{16,20},{20,16},{24,28},{28,24},{1,5},{5... | collective-permute-start | bytes 3551240 | tf_op jit(solution)/shard_map/ppermute | solution.py:580
  98.6 1.3 copy-start.3
  100.0 19.2 %collective-permute-start.9 = (f32[584,128]{1,0:T(8,128)S(1)}, f32[584,128]{1,0:T(8,128)S(1)}, u32[]{:S(2)}, u32[]{:S(2)}) collective-permute-start(f32[584,128]{1,0:T(8,128)S(1)} %get-tuple-element.95), channel_id=1, source_target_pairs={{1,0},{2,1},{3,2},{0,3},{5,4},{6,5},{7,6},{4,7},{9,8},{10,9},{11,1... | collective-permute-start | bytes 897032 | tf_op jit(solution)/shard_map/ppermute | solution.py:684
  102.7 21.5 %collective-permute-start.10 = (f32[584,128]{1,0:T(8,128)S(1)}, f32[584,128]{1,0:T(8,128)S(1)}, u32[]{:S(2)}, u32[]{:S(2)}) collective-permute-start(f32[584,128]{1,0:T(8,128)S(1)} %get-tuple-element.96), channel_id=1, source_target_pairs={{2,0},{3,1},{0,2},{1,3},{6,4},{7,5},{4,6},{5,7},{10,8},{11,9},{8,1... | collective-permute-start | bytes 897032 | tf_op jit(solution)/shard_map/ppermute | solution.py:684
  103.3 21.0 %collective-permute-start.11 = (f32[584,128]{1,0:T(8,128)S(1)}, f32[584,128]{1,0:T(8,128)S(1)}, u32[]{:S(2)}, u32[]{:S(2)}) collective-permute-start(f32[584,128]{1,0:T(8,128)S(1)} %get-tuple-element.97), channel_id=1, source_target_pairs={{3,0},{0,1},{1,2},{2,3},{7,4},{4,5},{5,6},{6,7},{11,8},{8,9},{9,10... | collective-permute-start | bytes 897032 | tf_op jit(solution)/shard_map/ppermute | solution.py:684
  103.9 6.7 %copy-start.13 = (f32[32,8,128]{2,1,0:T(8,128)S(1)}, f32[32,8,128]{2,1,0:T(8,128)}, u32[]{:S(2)}) copy-start(f32[32,8,128]{2,1,0:T(8,128)} %copy-done.12) | copy-start | bytes 393220
  119.2 17.8 %copy-start.6 = (f32[8,128]{1,0:T(8,128)S(1)}, f32[8,128]{1,0:T(8,128)}, u32[]{:S(2)}) copy-start(f32[8,128]{1,0:T(8,128)} %get-tuple-element.115.refs_4_) | copy-start | bytes 12292
  119.2 17.8 %collective-permute-start.15 = (f32[8,128]{1,0:T(8,128)}, f32[8,128]{1,0:T(8,128)S(1)}, u32[]{:S(2)}, u32[]{:S(2)}) collective-permute-start(f32[8,128]{1,0:T(8,128)} %get-tuple-element.115.refs_4_), channel_id=1, source_target_pairs={{0,4},{4,0},{8,12},{12,8},{16,20},{20,16},{24,28},{28,24},{1,5},{5... | collective-permute-start | bytes 12296 | tf_op jit(solution)/shard_map/ppermute | solution.py:580
  124.6 7.2 %collective-permute-start.12 = (f16[304,128]{1,0:T(8,128)(2,1)S(1)}, f16[304,128]{1,0:T(8,128)(2,1)S(1)}, u32[]{:S(2)}, u32[]{:S(2)}) collective-permute-start(f16[304,128]{1,0:T(8,128)(2,1)S(1)} %convert_element_type.66), channel_id=1, source_target_pairs={{8,0},{12,4},{16,8},{20,12},{24,16},{28,20},{0,24},{4,28},{9,1},{1... | collective-permute-start | bytes 233480 | tf_op jit(solution)/shard_map/ppermute | solution.py:698
  127.6 9.3 %collective-permute-start.13 = (f16[304,128]{1,0:T(8,128)(2,1)S(1)}, f16[304,128]{1,0:T(8,128)(2,1)S(1)}, u32[]{:S(2)}, u32[]{:S(2)}) collective-permute-start(f16[304,128]{1,0:T(8,128)(2,1)S(1)} %convert_element_type.68), channel_id=1, source_target_pairs={{16,0},{20,4},{24,8},{28,12},{0,16},{4,20},{8,24},{12,28},{17,1},{... | collective-permute-start | bytes 233480 | tf_op jit(solution)/shard_map/ppermute | solution.py:698
  129.8 7.1 %collective-permute-start.14 = (f16[304,128]{1,0:T(8,128)(2,1)S(1)}, f16[304,128]{1,0:T(8,128)(2,1)S(1)}, u32[]{:S(2)}, u32[]{:S(2)}) collective-permute-start(f16[304,128]{1,0:T(8,128)(2,1)S(1)} %convert_element_type.70), channel_id=1, source_target_pairs={{24,0},{28,4},{0,8},{4,12},{8,16},{12,20},{16,24},{20,28},{25,1},{... | collective-permute-start | bytes 233480 | tf_op jit(solution)/shard_map/ppermute | solution.py:698
  137.2 6.4 %collective-permute-start.18 = (f16[312,128]{1,0:T(8,128)(2,1)S(1)}, f16[312,128]{1,0:T(8,128)(2,1)S(1)}, u32[]{:S(2)}, u32[]{:S(2)}) collective-permute-start(f16[312,128]{1,0:T(8,128)(2,1)S(1)} %convert_element_type.74), channel_id=1, source_target_pairs={{24,0},{28,4},{0,8},{4,12},{8,16},{12,20},{16,24},{20,28},{25,1},{... | collective-permute-start | bytes 239624 | tf_op jit(solution)/shard_map/ppermute | solution.py:711
  137.2 7.5 %collective-permute-start.17 = (f16[312,128]{1,0:T(8,128)(2,1)S(1)}, f16[312,128]{1,0:T(8,128)(2,1)S(1)}, u32[]{:S(2)}, u32[]{:S(2)}) collective-permute-start(f16[312,128]{1,0:T(8,128)(2,1)S(1)} %convert_element_type.74), channel_id=1, source_target_pairs={{16,0},{20,4},{24,8},{28,12},{0,16},{4,20},{8,24},{12,28},{17,1},{... | collective-permute-start | bytes 239624 | tf_op jit(solution)/shard_map/ppermute | solution.py:711
  138.9 5.9 %collective-permute-start.16 = (f16[312,128]{1,0:T(8,128)(2,1)S(1)}, f16[312,128]{1,0:T(8,128)(2,1)S(1)}, u32[]{:S(2)}, u32[]{:S(2)}) collective-permute-start(f16[312,128]{1,0:T(8,128)(2,1)S(1)} %convert_element_type.74), channel_id=1, source_target_pairs={{8,0},{12,4},{16,8},{20,12},{24,16},{28,20},{0,24},{4,28},{9,1},{1... | collective-permute-start | bytes 239624 | tf_op jit(solution)/shard_map/ppermute | solution.py:711
  144.9 12.0 %collective-permute-start.19 = (f16[4,312,128]{2,1,0:T(8,128)(2,1)S(1)}, f16[4,312,128]{2,1,0:T(8,128)(2,1)S(1)}, u32[]{:S(2)}, u32[]{:S(2)}) collective-permute-start(f16[4,312,128]{2,1,0:T(8,128)(2,1)S(1)} %pad_maximum_fusion.3), channel_id=1, source_target_pairs={{1,0},{2,1},{3,2},{0,3},{5,4},{6,5},{7,6},{4,7},{9,8},{10,9},{11,1... | collective-permute-start | bytes 958472 | tf_op jit(solution)/shard_map/ppermute | solution.py:715
  149.0 13.4 %collective-permute-start.20 = (f16[4,312,128]{2,1,0:T(8,128)(2,1)S(1)}, f16[4,312,128]{2,1,0:T(8,128)(2,1)S(1)}, u32[]{:S(2)}, u32[]{:S(2)}) collective-permute-start(f16[4,312,128]{2,1,0:T(8,128)(2,1)S(1)} %pad_maximum_fusion.3), channel_id=1, source_target_pairs={{2,0},{3,1},{0,2},{1,3},{6,4},{7,5},{4,6},{5,7},{10,8},{11,9},{8,1... | collective-permute-start | bytes 958472 | tf_op jit(solution)/shard_map/ppermute | solution.py:715
  149.5 12.9 %collective-permute-start.21 = (f16[4,312,128]{2,1,0:T(8,128)(2,1)S(1)}, f16[4,312,128]{2,1,0:T(8,128)(2,1)S(1)}, u32[]{:S(2)}, u32[]{:S(2)}) collective-permute-start(f16[4,312,128]{2,1,0:T(8,128)(2,1)S(1)} %pad_maximum_fusion.3), channel_id=1, source_target_pairs={{3,0},{0,1},{1,2},{2,3},{7,4},{4,5},{5,6},{6,7},{11,8},{8,9},{9,10... | collective-permute-start | bytes 958472 | tf_op jit(solution)/shard_map/ppermute | solution.py:715
  152.0 11.7 %copy-start.1 = (f32[16,128,256]{2,1,0:T(8,128)S(1)}, f32[16,128,256]{2,1,0:T(8,128)}, u32[]{:S(2)}) copy-start(f32[16,128,256]{2,1,0:T(8,128)} %get-tuple-element.101.refs_1_) | copy-start | bytes 6291460
  155.1 8.5 %copy-start = (f32[2608,256]{1,0:T(8,128)S(1)}, f32[2608,256]{1,0:T(8,128)}, u32[]{:S(2)}) copy-start(f32[2608,256]{1,0:T(8,128)} %get-tuple-element.99.refs_1_.refs_2_) | copy-start | bytes 8011780
  155.1 8.5 %copy-start.2 = (bf16[16,128,256]{2,1,0:T(8,128)(2,1)S(1)}, bf16[16,128,256]{2,1,0:T(8,128)(2,1)}, u32[]{:S(2)}) copy-start(bf16[16,128,256]{2,1,0:T(8,128)(2,1)} %refs_0_.6) | copy-start | bytes 3145732
  155.1 8.6 %copy-start.5 = (f32[8,256]{1,0:T(8,128)S(1)}, f32[8,256]{1,0:T(8,128)}, u32[]{:S(2)}) copy-start(f32[8,256]{1,0:T(8,128)} %get-tuple-element.100.refs_2_.refs_3_) | copy-start | bytes 24580
  155.1 8.6 %copy-start.7 = (f32[256]{0:T(256)S(1)}, f32[256]{0:T(256)}, u32[]{:S(2)}) copy-start(f32[256]{0:T(256)} %param.10) | copy-start | bytes 3076
  162.4 3.8 %collective-permute-start.22 = (f16[4,312,128]{2,1,0:T(8,128)(2,1)S(1)}, f16[4,312,128]{2,1,0:T(8,128)(2,1)S(1)}, u32[]{:S(2)}, u32[]{:S(2)}) collective-permute-start(f16[4,312,128]{2,1,0:T(8,128)(2,1)S(1)} %pad_maximum_fusion.3), channel_id=1, source_target_pairs={{0,4},{4,0},{8,12},{12,8},{16,20},{20,16},{24,28},{28,24},{1,5},{5... | collective-permute-start | bytes 958472 | tf_op jit(solution)/shard_map/ppermute | solution.py:580
  162.4 3.9 %collective-permute-start.23 = (f16[4,312,128]{2,1,0:T(8,128)(2,1)S(1)}, f16[4,312,128]{2,1,0:T(8,128)(2,1)S(1)}, u32[]{:S(2)}, u32[]{:S(2)}) collective-permute-start(f16[4,312,128]{2,1,0:T(8,128)(2,1)S(1)} %collective-permute-done.19), channel_id=1, source_target_pairs={{0,4},{4,0},{8,12},{12,8},{16,20},{20,16},{24,28},{28,24},{1,5},{5... | collective-permute-start | bytes 958472 | tf_op jit(solution)/shard_map/ppermute | solution.py:580
  162.9 3.4 %collective-permute-start.24 = (f16[4,312,128]{2,1,0:T(8,128)(2,1)S(1)}, f16[4,312,128]{2,1,0:T(8,128)(2,1)S(1)}, u32[]{:S(2)}, u32[]{:S(2)}) collective-permute-start(f16[4,312,128]{2,1,0:T(8,128)(2,1)S(1)} %collective-permute-done.20), channel_id=1, source_target_pairs={{0,4},{4,0},{8,12},{12,8},{16,20},{20,16},{24,28},{28,24},{1,5},{5... | collective-permute-start | bytes 958472 | tf_op jit(solution)/shard_map/ppermute | solution.py:580
  162.9 3.5 %collective-permute-start.25 = (f16[4,312,128]{2,1,0:T(8,128)(2,1)S(1)}, f16[4,312,128]{2,1,0:T(8,128)(2,1)S(1)}, u32[]{:S(2)}, u32[]{:S(2)}) collective-permute-start(f16[4,312,128]{2,1,0:T(8,128)(2,1)S(1)} %collective-permute-done.21), channel_id=1, source_target_pairs={{0,4},{4,0},{8,12},{12,8},{16,20},{20,16},{24,28},{28,24},{1,5},{5... | collective-permute-start | bytes 958472 | tf_op jit(solution)/shard_map/ppermute | solution.py:580
where the time goes:
time: 170 us; the launch traced here: 169 us
  Pallas kernels  63.3 us (37%)
  starting transfers between devices  49.5 us (29%)
  waiting for transfers between devices  30 us (18%)
  local copies, waits for them, and re-layouts  20.6 us (12%)
  other arithmetic  4.4 us (3%)
    pallas_call x14, Pallas kernels, call(): pl.pallas_call(wrapped, in_specs=specs, out_specs=jax.tree.unflatten(jax....  63.3 us
    all_to_all x2, starting transfers between devices, exchange(): return lax.all_to_all(x, AXES, split_axis=0, concat_axis=0, tiled=True)  14.1 us
    gather x1, local copies, waits for them, and re-layouts, body(): quantized = codebook[code_ids]  11.1 us
    ppermute x6, starting transfers between devices, column_send(): lax.ppermute(x, 'col', p)  8.07 us
    ppermute x3, waiting for transfers between devices, gather_columns(): lax.ppermute(own, 'col', p)  7.29 us
    ppermute x3, starting transfers between devices, row_sums(): sent = [lax.ppermute(x, 'row', p) for x, p in zip(sent, shifts(depth, 2))]  7.2 us
    unnamed x38, local copies, waits for them, and re-layouts  6.36 us
    ppermute x7, waiting for transfers between devices, pair_swap(): return lax.ppermute(x, 'row', [(i, i ^ 1) for i in range(size)])  5.51 us
  transfers between devices with their start and end apart: 28, of which 10 were waited for; matrix products, arithmetic and copies ran while one was open for 3% of the time, Pallas kernels for 34%

commit v1 on v0

--- a/solution.py
+++ b/solution.py
@@ -125,13 +125,13 @@
     def add_row(r, total):
         return total + jnp.sum(lat[r].astype(F32), 0, keepdims=True)
 
-    mean = lax.fori_loop(0, height, add_row, jnp.zeros((1, channels), F32)) * (1.0 / count)
+    mean = lax.fori_loop(0, height, add_row, jnp.zeros((1, channels), F32), unroll=4) * (1.0 / count)
 
     def add_square(r, total):
         gap = lat[r].astype(F32) - mean
         return total + jnp.sum(gap * gap, 0, keepdims=True)
 
-    square = lax.fori_loop(0, height, add_square, jnp.zeros((1, channels), F32))
+    square = lax.fori_loop(0, height, add_square, jnp.zeros((1, channels), F32), unroll=4)
     half = width
     rows = [mean[:, :half], mean[:, half:], square[:, :half], square[:, half:]]
     for i, part in enumerate(rows):
@@ -187,15 +187,12 @@
 
 
 def spread(scr, wide, count, pitch, channels):
-    def one(r, _):
-        value = scr[pl.ds(pl.multiple_of(r * pitch, 8), pitch + 2 * SIDE), :]
-        at = pl.ds(pl.multiple_of(r * pitch, 16), pitch)
+    for r in range(count):
+        value = scr[r * pitch : (r + 1) * pitch + 2 * SIDE, :]
+        at = slice(r * pitch, (r + 1) * pitch)
         for j in range(3):
             start = SIDE + j - 1
             wide[at, j * channels : (j + 1) * channels] = value[start : start + pitch].astype(BF16)
-        return 0
-
-    lax.fori_loop(0, count, one, 0)
 
 
 def rows_at(r, pitch, count):
@@ -396,7 +393,7 @@
             packed[pl.ds(slots[i * 16 + u], 1), :] = value[u : u + 1, :]
         return 0
 
-    lax.fori_loop(0, pull.shape[0] // 16, some, 0)
+    lax.fori_loop(0, pull.shape[0] // 16, some, 0, unroll=2)
 
 
 def flip_weight(weight, flipped):
@@ -585,46 +582,7 @@
     return [[((i + s * stride) % size, i) for i in range(size)] for s in range(1, n)]
 
 
-def columns_kernel(cols, *refs):
-    ins, outs = refs[:-cols], refs[-cols:]
-    col = lax.axis_index("col")
-    extra = ins[0].shape[0] % 256
-    taps = ins[0].shape[0] - extra
-    lines = taps // cols
-    for s, out in enumerate(outs):
-        at = pl.ds(pl.multiple_of((col + cols - s) % cols * lines, 8), lines)
-        out[:lines, :] = ins[0][at, :] + ins[1][at, :]
-        if extra:
-            out[lines:, :] = ins[0][taps:, :] + ins[1][taps:, :]
-
-
-def rows_kernel(cols, *refs):
-    parts, outs = (refs[:cols], refs[cols : 2 * cols]), refs[2 * cols :]
-    row, _, rows, _ = place_of()
-    depth = rows // 2
-    lines = outs[0].shape[0] // 2 - 4
-
-    def added(some, first, count):
-        value = some[0][first : first + count, :]
-        for ref in some[1:]:
-            value = value + ref[first : first + count, :]
-        return value
-
-    tail = added(parts[0], depth * lines, 8)
-    tops = [jnp.zeros((1, tail.shape[1]), F32)] * 2
-    for z in range(depth):
-        values = [added(some, z * lines, lines) for some in parts]
-        tops = [
-            jnp.maximum(top, jnp.max(jnp.abs(some), 0, keepdims=True))
-            for top, some in zip(tops, values)
-        ]
-        for s, out in enumerate(outs):
-
-            @pl.when((row // 2 + depth - s) % depth == z)
-            def _():
-                for i in range(2):
-                    out[i * lines : (i + 1) * lines, :] = values[i]
-
+def finish(outs, lines, tail, tops):
     end = 2 * lines
     powers = [exponent(jnp.max(top, 1, keepdims=True)) for top in tops]
     outs[0][end:, :] = tail
@@ -635,6 +593,58 @@
             at = slice(i * lines, (i + 1) * lines)
             out[at, :] = out[at, :] * jnp.exp2(power)
             out[end + 8 + i : end + 9 + i, :] = jnp.broadcast_to(power, (1, tail.shape[1]))
+
+
+def columns_kernel(cols, enc, enc_b, dec, dec_b, *outs):
+    col = lax.axis_index("col")
+    taps = dec.shape[0]
+    lines = taps // cols
+    tops = [jnp.zeros((1, dec.shape[1]), F32)] * 2
+    for s, out in enumerate(outs):
+        at = pl.ds(pl.multiple_of((col + cols - s) % cols * lines, 8), lines)
+        for i, (one, two) in enumerate(((enc, enc_b), (dec, dec_b))):
+            some = one[at, :] + two[at, :]
+            out[i * lines : (i + 1) * lines, :] = some
+            tops[i] = jnp.maximum(tops[i], jnp.max(jnp.abs(some), 0, keepdims=True))
+    finish(outs, lines, enc[taps:, :] + enc_b[taps:, :], tops)
+
+
+def rows_kernel(cols, *refs):
+    parts, outs = refs[:cols], refs[cols:]
+    row, _, rows, _ = place_of()
+    depth = rows // 2
+    lines = outs[0].shape[0] // 2 - 4
+    wide = depth * lines
+    end = 2 * wide
+    scales = [
+        [jnp.exp2(-ref[end + 8 + i : end + 9 + i, :]) for ref in parts[1:]] for i in range(2)
+    ]
+
+    def added(i, first, count):
+        at = slice(i * wide + first, i * wide + first + count)
+        value = parts[0][at, :]
+        for ref, scale in zip(parts[1:], scales[i]):
+            value = value + ref[at, :] * scale
+        return value
+
+    tail = parts[0][end:, :]
+    for ref in parts[1:]:
+        tail = tail + ref[end : end + 8, :]
+    tops = [jnp.zeros((1, tail.shape[1]), F32)] * 2
+    for z in range(depth):
+        values = [added(i, z * lines, lines) for i in range(2)]
+        tops = [
+            jnp.maximum(top, jnp.max(jnp.abs(some), 0, keepdims=True))
+            for top, some in zip(tops, values)
+        ]
+        for s, out in enumerate(outs):
+
+            @pl.when((row // 2 + depth - s) % depth == z)
+            def _():
+                for i in range(2):
+                    out[i * lines : (i + 1) * lines, :] = values[i]
+
+    finish(outs, lines, tail, tops)
 
 
 def chunk_kernel(depth, *refs):
@@ -666,37 +676,38 @@
         out[end + i : end + i + 1, :] = jnp.broadcast_to(power, (1, half))
 
 
-def column_parts(arrays):
+def message_shapes(lines, half, count):
+    return [shaped((2 * lines + 8, half))] + [shaped((2 * lines + 16, half))] * (count - 1)
+
+
+def pass_on(parts, axis, perms):
+    sent = [lax.ppermute(x.astype(F16), axis, p) for x, p in zip(parts[1:], perms)]
+    return [parts[0]] + [x.astype(F32) for x in sent]
+
+
+def column_sums(arrays):
     cols = lax.axis_size("col")
-    taps, half = arrays[0].shape
-    extra = taps % 256
+    taps, half = arrays[2].shape
     parts = call(
         lambda *refs: columns_kernel(cols, *refs),
         arrays,
-        [shaped(((taps - extra) // cols + extra, half))] * cols,
-        moved=4 * 10**6,
-    )
-    return list(parts)
-
-
-def column_send(parts):
-    cols = lax.axis_size("col")
-    return [parts[0]] + [lax.ppermute(x, "col", p) for x, p in zip(parts[1:], shifts(cols))]
-
-
-def row_sums(enc, dec, tail):
-    cols, depth = len(enc), lax.axis_size("row") // 2
-    taps, half = dec[0].shape
-    lines = taps // depth
+        message_shapes(taps // cols, half, cols),
+        moved=8 * 10**6,
+    )
+    return pass_on(parts, "col", shifts(cols))
+
+
+def row_sums(parts, tail):
+    cols, depth = len(parts), lax.axis_size("row") // 2
+    half = parts[0].shape[1]
+    lines = (parts[0].shape[0] // 2 - 4) // depth
     parts = call(
         lambda *refs: rows_kernel(cols, *refs),
-        enc + dec,
-        [shaped((2 * lines + 8, half))] + [shaped((2 * lines + 16, half))] * (depth - 1),
+        parts,
+        message_shapes(lines, half, depth),
         moved=4 * 10**6,
     )
-    sent = [x.astype(F16) for x in parts[1:]]
-    sent = [lax.ppermute(x, "row", p) for x, p in zip(sent, shifts(depth, 2))]
-    parts = [parts[0]] + [x.astype(F32) for x in sent]
+    parts = pass_on(parts, "row", shifts(depth, 2))
     return call(
         lambda *refs: chunk_kernel(depth, *refs),
         parts + [tail, pair_swap(tail)],
@@ -820,9 +831,7 @@
     )
     dec_keep, dec_give = dec_grad
     gathered, dec_keep, dec_give = after(gathered, dec_keep, dec_give)
-    dec_parts = column_parts((dec_keep, pair_swap(dec_give)))
-    gathered, *dec_parts = after(gathered, *dec_parts)
-    dec_parts = column_send(dec_parts)
+    dec_given = pair_swap(dec_give)
     enc_fwd = encoder_weight.reshape(3, 3 * channels, channels)
     dec_fwd = decoder_weight.reshape(3, 3 * channels, channels)
     code_scale = codes_total / (count * devices)
@@ -859,7 +868,7 @@
         moved=6 * 10**6,
     )
     send = packed.astype(F16).reshape(devices, cap, channels)
-    send, z, *dec_parts = after(send, z, *dec_parts)
+    send, z, dec_given = after(send, z, dec_given)
     received = exchange(send)
 
     back_plane, keep_grad, give_grad = call(
@@ -890,7 +899,7 @@
             (0, None), *halos(1, 1), (5, None), *halos(2, 6), (12, None), (10, None), (11, None)
         ],
     )
-    enc_parts = column_send(column_parts((keep_grad, pair_swap(give_grad))))
+    parts = column_sums((keep_grad, pair_swap(give_grad), dec_keep, dec_given))
     back_act, tail = call(
         back_kernel,
         (latents, back_plane, stats, gain, bias, encoder_weight),
@@ -915,8 +924,8 @@
         moved=4 * 10**6,
         late=[(0, None), *halos(2, 1), (5, None)],
     )
-    decoded, *enc_parts = after(decoded, *enc_parts)
-    chunk, powers = row_sums(enc_parts, dec_parts, tail)
+    decoded, *parts = after(decoded, *parts)
+    chunk, powers = row_sums(parts, tail)
     own = gather_rows(chunk)
     pieces = gather_columns(own)
 

time: 170 us -> 162 us (0.953)
  starting transfers between devices: 49.5 us -> 44.2 us
    ppermute x9 -> x6, starting transfers between devices: 15.3 us -> 11.1 us  [pass_on(): lax.ppermute(x.astype(F16), axis, p)]
    ppermute x1, waiting for transfers between devices: 3.52 us -> 0.01 us  [halo(): right = lax.ppermute(left_edge, 'col', back(cols))]
    ppermute x3, waiting for transfers between devices: 3.6 us -> 6.08 us  [gather_rows(): return jnp.stack([own] + [lax.ppermute(own, 'row', p) for p in steps])]
    ppermute x7, waiting for transfers between devices: 5.51 us -> 3.04 us  [pair_swap(): return lax.ppermute(x, 'row', [(i, i ^ 1) for i in range(size)])]
    ppermute x1, starting transfers between devices: 1.32 us -> 3.06 us  [halo(): up = lax.ppermute(lines(slice(-HALO, None)), 'row', forth(rows))]
    ppermute x3, starting transfers between devices: 5.26 us -> 3.56 us  [gather_columns(): lax.ppermute(own, 'col', p)]
    pallas_call x14 -> x13, Pallas kernels: 63.3 us -> 62 us  [call(): pl.pallas_call(wrapped, in_specs=specs, out_specs=jax.tree.unflatten(jax....]
    ppermute x9 -> x6, waiting for transfers between devices: 10 us -> 10.5 us  [pass_on(): lax.ppermute(x.astype(F16), axis, p)]
  transfers between devices with their start and end apart: 28 -> 25, of which waited for: 10 -> 8; matrix products, arithmetic and copies ran while one was open for 3% -> 4% of each run, Pallas kernels for 34% -> 35%
where the time goes in v1:
time: 162 us; the launch traced here: 161 us
  Pallas kernels  62 us (38%)
  starting transfers between devices  44.2 us (27%)
  waiting for transfers between devices  28.8 us (18%)
  local copies, waits for them, and re-layouts  19.8 us (12%)
  other arithmetic  4.63 us (3%)
    pallas_call x13, Pallas kernels, call(): pl.pallas_call(wrapped, in_specs=specs, out_specs=jax.tree.unflatten(jax....  62 us
    all_to_all x2, starting transfers between devices, exchange(): return lax.all_to_all(x, AXES, split_axis=0, concat_axis=0, tiled=True)  14.5 us
    gather x1, local copies, waits for them, and re-layouts, body(): quantized = codebook[code_ids]  11.1 us
    ppermute x6, starting transfers between devices, pass_on(): lax.ppermute(x.astype(F16), axis, p)  11.1 us
    ppermute x6, waiting for transfers between devices, pass_on(): lax.ppermute(x.astype(F16), axis, p)  10.5 us
    ppermute x3, waiting for transfers between devices, gather_columns(): lax.ppermute(own, 'col', p)  8.7 us
    ppermute x3, waiting for transfers between devices, gather_rows(): return jnp.stack([own] + [lax.ppermute(own, 'row', p) for p in steps])  6.08 us
    unnamed x38, local copies, waits for them, and re-layouts  5.57 us
  transfers between devices with their start and end apart: 25, of which 8 were waited for; matrix products, arithmetic and copies ran while one was open for 4% of the time, Pallas kernels for 35%

profile of v1, /device:TPU:0, one launch (start us, length us, event | category | flops | bytes accessed | tf_op | source)
XLA Modules:
  0.0 160.7 jit_solution(12589966755416915859)
XLA Ops:
  0.6 3.2 %shard_map.135 = (f32[32,8,128]{2,1,0:T(8,128)}, s32[16,128]{1,0:T(8,128)}) custom-call(bf16[16,128,256]{2,1,0:T(8,128)(2,1)} %refs_0_.6, s32[16,128]{1,0:T(8,128)} %refs_1_.1), custom_call_target="tpu_custom_call" | custom-call | flops 1000000000 | bytes 1000000 | tf_op jit(solution)/shard_map/pallas_call | solution.py:61
  3.9 11.1 %gather_fusion = bf16[2048,256]{1,0:T(8,128)(2,1)S(1)} fusion(bf16[16384,256]{1,0:T(8,128)(2,1)} %param.13, s32[2048]{0:T(1024)S(1)} %fusion.3), kind=kCustom, calls=%fused_computation | custom fusion | bytes 2105344 | tf_op jit(solution)/shard_map/gather | solution.py:814
  15.0 0.0 copy-start.11
  15.0 1.3 slice_bitcast_fusion.6
  16.4 0.1 pad_maximum_fusion.5
  16.4 1.3 collective-permute-start.1
  17.7 0.1 pad_maximum_fusion.4
  17.8 5.5 %collective-permute-start = (bf16[3,16,2,256]{3,2,1,0:T(2,128)(2,1)S(1)}, bf16[3,16,2,256]{3,2,1,0:T(2,128)(2,1)S(1)}, u32[]{:S(2)}, u32[]{:S(2)}) collective-permute-start(bf16[3,16,2,256]{3,2,1,0:T(2,128)(2,1)S(1)} %pad_maximum_fusion.4), channel_id=1, source_target_pairs={{0,1},{1,2},{2,3},{4,5},{5,6},{6,7},{8,9},{9,10},{10,11},{12,13},{... | collective-permute-start | bytes 147464 | tf_op jit(solution)/shard_map/ppermute | solution.py:765
  23.3 1.1 slice_bitcast_fusion
  24.5 0.5 collective-permute-done.refs_1_.refs_2_.refs_6_
  25.1 0.1 pad_maximum_fusion.2
  25.2 1.3 collective-permute-start.3
  26.5 0.1 pad_maximum_fusion.1
  26.6 3.1 %collective-permute-start.2 = (bf16[3,2,132,256]{3,2,1,0:T(8,128)(2,1)S(1)}, bf16[3,2,132,256]{3,2,1,0:T(8,128)(2,1)S(1)}, u32[]{:S(2)}, u32[]{:S(2)}) collective-permute-start(bf16[3,2,132,256]{3,2,1,0:T(8,128)(2,1)S(1)} %pad_maximum_fusion.1), channel_id=1, source_target_pairs={{0,4},{4,8},{8,12},{12,16},{16,20},{20,24},{24,28},{1,5},{5,9},{9,... | collective-permute-start | bytes 1216520 | tf_op jit(solution)/shard_map/ppermute | solution.py:771
  29.7 8.3 %all-to-all-start = ((f32[32,8,128]{2,1,0:T(8,128)}), f32[32,8,128]{2,1,0:T(8,128)S(1)}, u32[]{:S(2)}, u32[]{:S(2)}) async-start(f32[32,8,128]{2,1,0:T(8,128)} %get-tuple-element.60), calls=%async_computation | async-start | bytes 262144 | tf_op jit(solution)/shard_map/all_to_all | solution.py:572
  38.0 0.7 copy-done.17
  38.7 0.8 copy-done.18
  39.5 6.7 %shard_map.137 = (f32[2304,128]{1,0:T(8,128)}, f32[2304,128]{1,0:T(8,128)}) custom-call(bf16[16,128,256]{2,1,0:T(8,128)(2,1)} %refs_0_.4, bf16[16,128,256]{2,1,0:T(8,128)(2,1)} %bitcast.54, bf16[3,16,2,256]{3,2,1,0:T(2,128)(2,1)} %copy-done.16, bf16[3,16,2,256]{3,2,1,0:T(2,128)(2,1)} %copy-done.15, bf16[3,2,132,256]{3,2,1,0:T(8,128)(2,1)} %copy-done.18, ...), custom_call_target="tpu_custom_call" | custom-call | flops 2415919104 | bytes 5000000 | tf_op jit(solution)/shard_map/pallas_call | solution.py:61
  46.2 0.1 collective-permute-start.4
  46.4 0.5 copy-done.12
  46.9 10.0 %shard_map.138 = (f32[2608,256]{1,0:T(8,128)}, f32[2048,256]{1,0:T(8,128)}, bf16[256,2304]{1,0:T(8,128)(2,1)}, f32[8,256]{1,0:T(8,128)}, f32[8,256]{1,0:T(8,128)}) custom-call(bf16[16,128,256]{2,1,0:T(8,128)(2,1)} %refs_0_.6, bf16[3,16,2,256]{3,2,1,0:T(2,128)(2,1)} %copy-done.16, bf16[3,16,2,256]{3,2,1,0:T(2,128)(2,1)} %copy-done.15, ...), custom_call_target="tpu_custom_call" | custom-call | flops 2415919104 | bytes 10000000 | tf_op jit(solution)/shard_map/pallas_call | solution.py:61
  56.9 1.6 copy-done.9
  58.5 0.7 copy-done.10
  59.2 5.4 %shard_map.139 = f32[4096,256]{1,0:T(8,128)S(1)} custom-call(s32[2048]{0:T(1024)S(1)} %bitcast.52, f32[2048,256]{1,0:T(8,128)S(1)} %copy-done.9, f32[8,256]{1,0:T(8,128)S(1)} %copy-done.10), custom_call_target="tpu_custom_call" | custom-call | flops 5000000000 | bytes 6000000 | tf_op jit(solution)/shard_map/pallas_call | solution.py:61
  64.6 1.6 convert_element_type.80
  66.2 6.2 %all-to-all-start.1 = ((f16[32,128,256]{2,1,0:T(8,128)(2,1)}), f16[32,128,256]{2,1,0:T(8,128)(2,1)S(1)}, u32[]{:S(2)}, u32[]{:S(2)}) async-start(f16[32,128,256]{2,1,0:T(8,128)(2,1)} %bitcast.19), calls=%async_computation.1 | async-start | bytes 4194304 | tf_op jit(solution)/shard_map/all_to_all | solution.py:572
  72.5 12.8 %shard_map.140 = (f32[2608,256]{1,0:T(8,128)}, f32[2312,128]{1,0:T(8,128)}, f32[2312,128]{1,0:T(8,128)}) custom-call(bf16[16,128,256]{2,1,0:T(8,128)(2,1)} %refs_0_.4, bf16[3,16,2,256]{3,2,1,0:T(2,128)(2,1)} %copy-done.16, bf16[3,16,2,256]{3,2,1,0:T(2,128)(2,1)} %copy-done.15, bf16[3,2,132,256]{3,2,1,0:T(8,128)(2,1)} %copy-done.18, ...), custom_call_target="tpu_custom_call" | custom-call | flops 4831838208 | bytes 15000000 | tf_op jit(solution)/shard_map/pallas_call | solution.py:61
  85.2 0.1 collective-permute-start.5
  85.3 3.0 %collective-permute-done.5.refs_1_ = f32[2312,128]{1,0:T(8,128)S(1)} collective-permute-done((f32[2312,128]{1,0:T(8,128)}, f32[2312,128]{1,0:T(8,128)S(1)}, u32[]{:S(2)}, u32[]{:S(2)}) %collective-permute-start.5) | collective-permute-done | bytes 1183776 | tf_op jit(solution)/shard_map/ppermute | solution.py:577
  88.4 1.3 copy-done.3
  89.6 0.5 shard_map.141
  90.2 2.5 %collective-permute-start.6 = (f16[1168,128]{1,0:T(8,128)(2,1)S(1)}, f16[1168,128]{1,0:T(8,128)(2,1)S(1)}, u32[]{:S(2)}, u32[]{:S(2)}) collective-permute-start(f16[1168,128]{1,0:T(8,128)(2,1)S(1)} %convert_element_type.81), channel_id=1, source_target_pairs={{1,0},{2,1},{3,2},{0,3},{5,4},{6,5},{7,6},{4,7},{9,8},{10,9},{11,1... | collective-permute-start | bytes 897032 | tf_op jit(solution)/shard_map/ppermute | solution.py:684
  92.8 0.6 collective-permute-start.7
  93.5 0.9 collective-permute-start.8
  94.3 6.6 %shard_map.136 = bf16[16,128,256]{2,1,0:T(8,128)(2,1)} custom-call(bf16[16,128,256]{2,1,0:T(8,128)(2,1)} %bitcast.57, bf16[3,16,2,256]{3,2,1,0:T(2,128)(2,1)} %copy-done.16, bf16[3,16,2,256]{3,2,1,0:T(2,128)(2,1)} %copy-done.15, bf16[3,2,132,256]{3,2,1,0:T(8,128)(2,1)} %copy-done.18, bf16[3,2,132,256]{3,2,1,0:T(8,128)(2,1)} %copy-done.17, ...), custom_call_target="tpu_custom_call" | custom-call | flops 2415919104 | bytes 4000000 | tf_op jit(solution)/shard_map/pallas_call | solution.py:61
  101.0 8.4 %shard_map.142 = (f32[16,128,256]{2,1,0:T(8,128)}, f32[8,128]{1,0:T(8,128)}) custom-call(bf16[16,128,256]{2,1,0:T(8,128)(2,1)} %refs_0_.6, f32[2608,256]{1,0:T(8,128)} %get-tuple-element.79.refs_1_.refs_2_, f32[8,256]{1,0:T(8,128)} %get-tuple-element.80.refs_2_.refs_3_, f32[1,256]{1,0:T(1,128)} %bitcast.50, f32[1,256]{1,0:T(1,128)} %bitcast.70, ...), custom_call_target="tpu_custom_call" | custom-call | flops 2415919104 | bytes 8000000 | tf_op jit(solution)/shard_map/pallas_call | solution.py:61
  109.4 0.1 collective-permute-start.12
  109.5 4.9 %collective-permute-done.7 = f16[1168,128]{1,0:T(8,128)(2,1)S(1)} collective-permute-done((f16[1168,128]{1,0:T(8,128)(2,1)S(1)}, f16[1168,128]{1,0:T(8,128)(2,1)S(1)}, u32[]{:S(2)}, u32[]{:S(2)}) %collective-permute-start.7) | collective-permute-done | bytes 299040 | tf_op jit(solution)/shard_map/ppermute | solution.py:684
  114.6 0.4 shard_map.143
  115.0 2.8 %collective-permute-start.9 = (f16[304,128]{1,0:T(8,128)(2,1)S(1)}, f16[304,128]{1,0:T(8,128)(2,1)S(1)}, u32[]{:S(2)}, u32[]{:S(2)}) collective-permute-start(f16[304,128]{1,0:T(8,128)(2,1)S(1)} %convert_element_type.90), channel_id=1, source_target_pairs={{8,0},{12,4},{16,8},{20,12},{24,16},{28,20},{0,24},{4,28},{9,1},{1... | collective-permute-start | bytes 233480 | tf_op jit(solution)/shard_map/ppermute | solution.py:684
  117.8 2.2 %collective-permute-start.10 = (f16[304,128]{1,0:T(8,128)(2,1)S(1)}, f16[304,128]{1,0:T(8,128)(2,1)S(1)}, u32[]{:S(2)}, u32[]{:S(2)}) collective-permute-start(f16[304,128]{1,0:T(8,128)(2,1)S(1)} %convert_element_type.92), channel_id=1, source_target_pairs={{16,0},{20,4},{24,8},{28,12},{0,16},{4,20},{8,24},{12,28},{17,1},{... | collective-permute-start | bytes 233480 | tf_op jit(solution)/shard_map/ppermute | solution.py:684
  120.0 2.1 %collective-permute-start.11 = (f16[304,128]{1,0:T(8,128)(2,1)S(1)}, f16[304,128]{1,0:T(8,128)(2,1)S(1)}, u32[]{:S(2)}, u32[]{:S(2)}) collective-permute-start(f16[304,128]{1,0:T(8,128)(2,1)S(1)} %convert_element_type.94), channel_id=1, source_target_pairs={{24,0},{28,4},{0,8},{4,12},{8,16},{12,20},{16,24},{20,28},{25,1},{... | collective-permute-start | bytes 233480 | tf_op jit(solution)/shard_map/ppermute | solution.py:684
  122.1 5.5 %collective-permute-done.10 = f16[304,128]{1,0:T(8,128)(2,1)S(1)} collective-permute-done((f16[304,128]{1,0:T(8,128)(2,1)S(1)}, f16[304,128]{1,0:T(8,128)(2,1)S(1)}, u32[]{:S(2)}, u32[]{:S(2)}) %collective-permute-start.10) | collective-permute-done | bytes 77856 | tf_op jit(solution)/shard_map/ppermute | solution.py:684
  127.7 0.2 shard_map.144
  127.9 0.6 collective-permute-start.13
  128.5 0.3 collective-permute-start.14
  128.8 1.7 %collective-permute-start.15 = (f16[312,128]{1,0:T(8,128)(2,1)S(1)}, f16[312,128]{1,0:T(8,128)(2,1)S(1)}, u32[]{:S(2)}, u32[]{:S(2)}) collective-permute-start(f16[312,128]{1,0:T(8,128)(2,1)S(1)} %convert_element_type.98), channel_id=1, source_target_pairs={{24,0},{28,4},{0,8},{4,12},{8,16},{12,20},{16,24},{20,28},{25,1},{... | collective-permute-start | bytes 239624 | tf_op jit(solution)/shard_map/ppermute | solution.py:722
  130.6 2.4 %collective-permute-done.13 = f16[312,128]{1,0:T(8,128)(2,1)S(1)} collective-permute-done((f16[312,128]{1,0:T(8,128)(2,1)S(1)}, f16[312,128]{1,0:T(8,128)(2,1)S(1)}, u32[]{:S(2)}, u32[]{:S(2)}) %collective-permute-start.13) | collective-permute-done | bytes 79904 | tf_op jit(solution)/shard_map/ppermute | solution.py:722
  132.9 3.7 %collective-permute-done.14 = f16[312,128]{1,0:T(8,128)(2,1)S(1)} collective-permute-done((f16[312,128]{1,0:T(8,128)(2,1)S(1)}, f16[312,128]{1,0:T(8,128)(2,1)S(1)}, u32[]{:S(2)}, u32[]{:S(2)}) %collective-permute-start.14) | collective-permute-done | bytes 79904 | tf_op jit(solution)/shard_map/ppermute | solution.py:722
  136.6 0.1 pad_maximum_fusion.3
  136.8 2.7 %collective-permute-start.16 = (f16[4,312,128]{2,1,0:T(8,128)(2,1)S(1)}, f16[4,312,128]{2,1,0:T(8,128)(2,1)S(1)}, u32[]{:S(2)}, u32[]{:S(2)}) collective-permute-start(f16[4,312,128]{2,1,0:T(8,128)(2,1)S(1)} %pad_maximum_fusion.3), channel_id=1, source_target_pairs={{1,0},{2,1},{3,2},{0,3},{5,4},{6,5},{7,6},{4,7},{9,8},{10,9},{11,1... | collective-permute-start | bytes 958472 | tf_op jit(solution)/shard_map/ppermute | solution.py:726
  139.5 0.2 collective-permute-start.17
  139.7 0.6 collective-permute-start.18
  140.3 0.6 convert_multiply_fusion
  140.9 0.9 reduce-precision_convert_fusion
  141.8 0.3 pad_maximum_fusion.refs_1_
  142.2 3.1 %shard_map.145 = f32[512,256]{1,0:T(8,128)} custom-call(s32[32,128]{1,0:T(8,128)S(1)} %fusion.1.refs_0_, bf16[4096,512]{1,0:T(8,128)(2,1)S(1)} %pad_maximum_fusion.refs_1_), custom_call_target="tpu_custom_call" | custom-call | flops 2000000000 | bytes 6000000 | tf_op jit(solution)/shard_map/pallas_call | solution.py:61
  145.3 2.2 %collective-permute-done.16 = f16[4,312,128]{2,1,0:T(8,128)(2,1)S(1)} collective-permute-done((f16[4,312,128]{2,1,0:T(8,128)(2,1)S(1)}, f16[4,312,128]{2,1,0:T(8,128)(2,1)S(1)}, u32[]{:S(2)}, u32[]{:S(2)}) %collective-permute-start.16) | collective-permute-done | bytes 319520 | tf_op jit(solution)/shard_map/ppermute | solution.py:726
  147.5 6.5 %collective-permute-done.17 = f16[4,312,128]{2,1,0:T(8,128)(2,1)S(1)} collective-permute-done((f16[4,312,128]{2,1,0:T(8,128)(2,1)S(1)}, f16[4,312,128]{2,1,0:T(8,128)(2,1)S(1)}, u32[]{:S(2)}, u32[]{:S(2)}) %collective-permute-start.17) | collective-permute-done | bytes 319520 | tf_op jit(solution)/shard_map/ppermute | solution.py:726
  154.0 0.5 collective-permute-start.20
  154.5 0.5 collective-permute-start.22
  155.3 2.0 %shard_map.146 = (bf16[16,128,256]{2,1,0:T(8,128)(2,1)}, f32[2,256]{1,0:T(2,128)S(1)}) custom-call(bf16[16,128,256]{2,1,0:T(8,128)(2,1)S(1)} %copy-done.2, f32[16,128,256]{2,1,0:T(8,128)S(1)} %copy-done.1, f32[2608,256]{1,0:T(8,128)S(1)} %copy-done, f32[8,256]{1,0:T(8,128)S(1)} %copy-done.5, f32[1,256]{1,0:T(1,128)S(1)} %bitcast.51, ...), custom_call_target="tpu_custom_call" | custom-call | flops 100000000 | bytes 6000000 | tf_op jit(solution)/shard_map/pallas_call | solution.py:61
  157.3 0.6 fusion.7
  158.1 2.6 %shard_map.147 = (f32[16,144,256]{2,1,0:T(8,128)}, f32[16,144,256]{2,1,0:T(8,128)}) custom-call(f32[4,312,128]{2,1,0:T(8,128)S(1)} %convert_element_type.99.refs_5_.refs_0_, f32[4,312,128]{2,1,0:T(8,128)S(1)} %convert_element_type.100.refs_6_.refs_1_, f32[4,312,128]{2,1,0:T(8,128)S(1)} %convert_element_type.101.refs_7_.refs_2_, ...), custom_call_target="tpu_custom_call" | custom-call | bytes 10000000 | tf_op jit(solution)/shard_map/pallas_call | solution.py:61
  (80 shorter events, 0.9 us)
Async XLA Ops:
  0.6 3.2 %copy-start.14 = (s32[16,128]{1,0:T(8,128)S(1)}, s32[16,128]{1,0:T(8,128)}, u32[]{:S(2)}) copy-start(s32[16,128]{1,0:T(8,128)} %refs_1_.1) | copy-start | bytes 24580
  15.0 23.0 %copy-start.11 = (bf16[2048,256]{1,0:T(8,128)(2,1)}, bf16[2048,256]{1,0:T(8,128)(2,1)S(1)}, u32[]{:S(2)}) copy-start(bf16[2048,256]{1,0:T(8,128)(2,1)S(1)} %gather_fusion) | copy-start | bytes 3145732
  16.4 8.0 %collective-permute-start.1 = (bf16[3,16,2,256]{3,2,1,0:T(2,128)(2,1)S(1)}, bf16[3,16,2,256]{3,2,1,0:T(2,128)(2,1)S(1)}, u32[]{:S(2)}, u32[]{:S(2)}) collective-permute-start(bf16[3,16,2,256]{3,2,1,0:T(2,128)(2,1)S(1)} %pad_maximum_fusion.5), channel_id=1, source_target_pairs={{1,0},{2,1},{3,2},{5,4},{6,5},{7,6},{9,8},{10,9},{11,10},{13,12},{... | collective-permute-start | bytes 147464 | tf_op jit(solution)/shard_map/ppermute | solution.py:766
  17.8 7.2 %collective-permute-start = (bf16[3,16,2,256]{3,2,1,0:T(2,128)(2,1)S(1)}, bf16[3,16,2,256]{3,2,1,0:T(2,128)(2,1)S(1)}, u32[]{:S(2)}, u32[]{:S(2)}) collective-permute-start(bf16[3,16,2,256]{3,2,1,0:T(2,128)(2,1)S(1)} %pad_maximum_fusion.4), channel_id=1, source_target_pairs={{0,1},{1,2},{2,3},{4,5},{5,6},{6,7},{8,9},{9,10},{10,11},{12,13},{... | collective-permute-start | bytes 147464 | tf_op jit(solution)/shard_map/ppermute | solution.py:765
  24.5 13.5 %copy-start.15 = (bf16[3,16,2,256]{3,2,1,0:T(2,128)(2,1)}, bf16[3,16,2,256]{3,2,1,0:T(2,128)(2,1)S(1)}, u32[]{:S(2)}) copy-start(bf16[3,16,2,256]{3,2,1,0:T(2,128)(2,1)S(1)} %collective-permute-done.1.refs_2_.refs_3_.refs_7_) | copy-start | bytes 147460
  25.0 13.0 %copy-start.16 = (bf16[3,16,2,256]{3,2,1,0:T(2,128)(2,1)}, bf16[3,16,2,256]{3,2,1,0:T(2,128)(2,1)S(1)}, u32[]{:S(2)}) copy-start(bf16[3,16,2,256]{3,2,1,0:T(2,128)(2,1)S(1)} %collective-permute-done.refs_1_.refs_2_.refs_6_) | copy-start | bytes 147460
  25.2 12.8 %collective-permute-start.3 = (bf16[3,2,132,256]{3,2,1,0:T(8,128)(2,1)S(1)}, bf16[3,2,132,256]{3,2,1,0:T(8,128)(2,1)S(1)}, u32[]{:S(2)}, u32[]{:S(2)}) collective-permute-start(bf16[3,2,132,256]{3,2,1,0:T(8,128)(2,1)S(1)} %pad_maximum_fusion.2), channel_id=1, source_target_pairs={{4,0},{8,4},{12,8},{16,12},{20,16},{24,20},{28,24},{5,1},{9,5},{13... | collective-permute-start | bytes 1216520 | tf_op jit(solution)/shard_map/ppermute | solution.py:772
  26.6 11.4 %collective-permute-start.2 = (bf16[3,2,132,256]{3,2,1,0:T(8,128)(2,1)S(1)}, bf16[3,2,132,256]{3,2,1,0:T(8,128)(2,1)S(1)}, u32[]{:S(2)}, u32[]{:S(2)}) collective-permute-start(bf16[3,2,132,256]{3,2,1,0:T(8,128)(2,1)S(1)} %pad_maximum_fusion.1), channel_id=1, source_target_pairs={{0,4},{4,8},{8,12},{12,16},{16,20},{20,24},{24,28},{1,5},{5,9},{9,... | collective-permute-start | bytes 1216520 | tf_op jit(solution)/shard_map/ppermute | solution.py:771
  29.7 16.5 %all-to-all-start = ((f32[32,8,128]{2,1,0:T(8,128)}), f32[32,8,128]{2,1,0:T(8,128)S(1)}, u32[]{:S(2)}, u32[]{:S(2)}) async-start(f32[32,8,128]{2,1,0:T(8,128)} %get-tuple-element.60), calls=%async_computation | async-start | bytes 262144 | tf_op jit(solution)/shard_map/all_to_all | solution.py:572
  38.0 0.8 copy-start.17
  38.7 0.8 copy-start.18
  46.2 0.6 copy-start.12
  46.2 20.0 %collective-permute-start.4 = (f32[2304,128]{1,0:T(8,128)}, f32[2304,128]{1,0:T(8,128)S(1)}, u32[]{:S(2)}, u32[]{:S(2)}) collective-permute-start(f32[2304,128]{1,0:T(8,128)} %get-tuple-element.67), channel_id=1, source_target_pairs={{0,4},{4,0},{8,12},{12,8},{16,20},{20,16},{24,28},{28,24},{1,5},{5... | collective-permute-start | bytes 3538952 | tf_op jit(solution)/shard_map/ppermute | solution.py:577
  46.9 10.0 %copy-start.8 = (s32[16,128]{1,0:T(8,128)S(1)}, s32[16,128]{1,0:T(8,128)}, u32[]{:S(2)}) copy-start(s32[16,128]{1,0:T(8,128)} %get-tuple-element.59) | copy-start | bytes 24580
  56.9 1.6 copy-start.9
  58.5 0.7 copy-start.10
  66.2 74.1 %all-to-all-start.1 = ((f16[32,128,256]{2,1,0:T(8,128)(2,1)}), f16[32,128,256]{2,1,0:T(8,128)(2,1)S(1)}, u32[]{:S(2)}, u32[]{:S(2)}) async-start(f16[32,128,256]{2,1,0:T(8,128)(2,1)} %bitcast.19), calls=%async_computation.1 | async-start | bytes 4194304 | tf_op jit(solution)/shard_map/all_to_all | solution.py:572
  72.4 15.9 %copy-start.4 = (f32[2304,128]{1,0:T(8,128)S(1)}, f32[2304,128]{1,0:T(8,128)}, u32[]{:S(2)}) copy-start(f32[2304,128]{1,0:T(8,128)} %get-tuple-element.72.refs_2_) | copy-start | bytes 3538948
  85.2 3.1 %collective-permute-start.5 = (f32[2312,128]{1,0:T(8,128)}, f32[2312,128]{1,0:T(8,128)S(1)}, u32[]{:S(2)}, u32[]{:S(2)}) collective-permute-start(f32[2312,128]{1,0:T(8,128)} %get-tuple-element.71), channel_id=1, source_target_pairs={{0,4},{4,0},{8,12},{12,8},{16,20},{20,16},{24,28},{28,24},{1,5},{5... | collective-permute-start | bytes 3551240 | tf_op jit(solution)/shard_map/ppermute | solution.py:577
  88.4 1.3 copy-start.3
  90.2 19.2 %collective-permute-start.6 = (f16[1168,128]{1,0:T(8,128)(2,1)S(1)}, f16[1168,128]{1,0:T(8,128)(2,1)S(1)}, u32[]{:S(2)}, u32[]{:S(2)}) collective-permute-start(f16[1168,128]{1,0:T(8,128)(2,1)S(1)} %convert_element_type.81), channel_id=1, source_target_pairs={{1,0},{2,1},{3,2},{0,3},{5,4},{6,5},{7,6},{4,7},{9,8},{10,9},{11,1... | collective-permute-start | bytes 897032 | tf_op jit(solution)/shard_map/ppermute | solution.py:684
  92.8 21.7 %collective-permute-start.7 = (f16[1168,128]{1,0:T(8,128)(2,1)S(1)}, f16[1168,128]{1,0:T(8,128)(2,1)S(1)}, u32[]{:S(2)}, u32[]{:S(2)}) collective-permute-start(f16[1168,128]{1,0:T(8,128)(2,1)S(1)} %convert_element_type.83), channel_id=1, source_target_pairs={{2,0},{3,1},{0,2},{1,3},{6,4},{7,5},{4,6},{5,7},{10,8},{11,9},{8,1... | collective-permute-start | bytes 897032 | tf_op jit(solution)/shard_map/ppermute | solution.py:684
  93.5 21.1 %collective-permute-start.8 = (f16[1168,128]{1,0:T(8,128)(2,1)S(1)}, f16[1168,128]{1,0:T(8,128)(2,1)S(1)}, u32[]{:S(2)}, u32[]{:S(2)}) collective-permute-start(f16[1168,128]{1,0:T(8,128)(2,1)S(1)} %convert_element_type.85), channel_id=1, source_target_pairs={{3,0},{0,1},{1,2},{2,3},{7,4},{4,5},{5,6},{6,7},{11,8},{8,9},{9,10... | collective-permute-start | bytes 897032 | tf_op jit(solution)/shard_map/ppermute | solution.py:684
  94.3 6.6 %copy-start.13 = (f32[32,8,128]{2,1,0:T(8,128)S(1)}, f32[32,8,128]{2,1,0:T(8,128)}, u32[]{:S(2)}) copy-start(f32[32,8,128]{2,1,0:T(8,128)} %copy-done.12) | copy-start | bytes 393220
  109.4 18.3 %collective-permute-start.12 = (f32[8,128]{1,0:T(8,128)}, f32[8,128]{1,0:T(8,128)S(1)}, u32[]{:S(2)}, u32[]{:S(2)}) collective-permute-start(f32[8,128]{1,0:T(8,128)} %get-tuple-element.91.refs_4_), channel_id=1, source_target_pairs={{0,4},{4,0},{8,12},{12,8},{16,20},{20,16},{24,28},{28,24},{1,5},{5... | collective-permute-start | bytes 12296 | tf_op jit(solution)/shard_map/ppermute | solution.py:577
  114.5 13.2 %copy-start.6 = (f32[8,128]{1,0:T(8,128)S(1)}, f32[8,128]{1,0:T(8,128)}, u32[]{:S(2)}) copy-start(f32[8,128]{1,0:T(8,128)} %get-tuple-element.91.refs_4_) | copy-start | bytes 12292
  115.0 7.1 %collective-permute-start.9 = (f16[304,128]{1,0:T(8,128)(2,1)S(1)}, f16[304,128]{1,0:T(8,128)(2,1)S(1)}, u32[]{:S(2)}, u32[]{:S(2)}) collective-permute-start(f16[304,128]{1,0:T(8,128)(2,1)S(1)} %convert_element_type.90), channel_id=1, source_target_pairs={{8,0},{12,4},{16,8},{20,12},{24,16},{28,20},{0,24},{4,28},{9,1},{1... | collective-permute-start | bytes 233480 | tf_op jit(solution)/shard_map/ppermute | solution.py:684
  117.8 9.9 %collective-permute-start.10 = (f16[304,128]{1,0:T(8,128)(2,1)S(1)}, f16[304,128]{1,0:T(8,128)(2,1)S(1)}, u32[]{:S(2)}, u32[]{:S(2)}) collective-permute-start(f16[304,128]{1,0:T(8,128)(2,1)S(1)} %convert_element_type.92), channel_id=1, source_target_pairs={{16,0},{20,4},{24,8},{28,12},{0,16},{4,20},{8,24},{12,28},{17,1},{... | collective-permute-start | bytes 233480 | tf_op jit(solution)/shard_map/ppermute | solution.py:684
  120.0 7.7 %collective-permute-start.11 = (f16[304,128]{1,0:T(8,128)(2,1)S(1)}, f16[304,128]{1,0:T(8,128)(2,1)S(1)}, u32[]{:S(2)}, u32[]{:S(2)}) collective-permute-start(f16[304,128]{1,0:T(8,128)(2,1)S(1)} %convert_element_type.94), channel_id=1, source_target_pairs={{24,0},{28,4},{0,8},{4,12},{8,16},{12,20},{16,24},{20,28},{25,1},{... | collective-permute-start | bytes 233480 | tf_op jit(solution)/shard_map/ppermute | solution.py:684
  127.9 5.0 %collective-permute-start.13 = (f16[312,128]{1,0:T(8,128)(2,1)S(1)}, f16[312,128]{1,0:T(8,128)(2,1)S(1)}, u32[]{:S(2)}, u32[]{:S(2)}) collective-permute-start(f16[312,128]{1,0:T(8,128)(2,1)S(1)} %convert_element_type.98), channel_id=1, source_target_pairs={{8,0},{12,4},{16,8},{20,12},{24,16},{28,20},{0,24},{4,28},{9,1},{1... | collective-permute-start | bytes 239624 | tf_op jit(solution)/shard_map/ppermute | solution.py:722
  128.5 8.1 %collective-permute-start.14 = (f16[312,128]{1,0:T(8,128)(2,1)S(1)}, f16[312,128]{1,0:T(8,128)(2,1)S(1)}, u32[]{:S(2)}, u32[]{:S(2)}) collective-permute-start(f16[312,128]{1,0:T(8,128)(2,1)S(1)} %convert_element_type.98), channel_id=1, source_target_pairs={{16,0},{20,4},{24,8},{28,12},{0,16},{4,20},{8,24},{12,28},{17,1},{... | collective-permute-start | bytes 239624 | tf_op jit(solution)/shard_map/ppermute | solution.py:722
  128.8 7.8 %collective-permute-start.15 = (f16[312,128]{1,0:T(8,128)(2,1)S(1)}, f16[312,128]{1,0:T(8,128)(2,1)S(1)}, u32[]{:S(2)}, u32[]{:S(2)}) collective-permute-start(f16[312,128]{1,0:T(8,128)(2,1)S(1)} %convert_element_type.98), channel_id=1, source_target_pairs={{24,0},{28,4},{0,8},{4,12},{8,16},{12,20},{16,24},{20,28},{25,1},{... | collective-permute-start | bytes 239624 | tf_op jit(solution)/shard_map/ppermute | solution.py:722
  136.8 10.7 %collective-permute-start.16 = (f16[4,312,128]{2,1,0:T(8,128)(2,1)S(1)}, f16[4,312,128]{2,1,0:T(8,128)(2,1)S(1)}, u32[]{:S(2)}, u32[]{:S(2)}) collective-permute-start(f16[4,312,128]{2,1,0:T(8,128)(2,1)S(1)} %pad_maximum_fusion.3), channel_id=1, source_target_pairs={{1,0},{2,1},{3,2},{0,3},{5,4},{6,5},{7,6},{4,7},{9,8},{10,9},{11,1... | collective-permute-start | bytes 958472 | tf_op jit(solution)/shard_map/ppermute | solution.py:726
  139.5 14.5 %collective-permute-start.17 = (f16[4,312,128]{2,1,0:T(8,128)(2,1)S(1)}, f16[4,312,128]{2,1,0:T(8,128)(2,1)S(1)}, u32[]{:S(2)}, u32[]{:S(2)}) collective-permute-start(f16[4,312,128]{2,1,0:T(8,128)(2,1)S(1)} %pad_maximum_fusion.3), channel_id=1, source_target_pairs={{2,0},{3,1},{0,2},{1,3},{6,4},{7,5},{4,6},{5,7},{10,8},{11,9},{8,1... | collective-permute-start | bytes 958472 | tf_op jit(solution)/shard_map/ppermute | solution.py:726
  139.7 14.3 %collective-permute-start.18 = (f16[4,312,128]{2,1,0:T(8,128)(2,1)S(1)}, f16[4,312,128]{2,1,0:T(8,128)(2,1)S(1)}, u32[]{:S(2)}, u32[]{:S(2)}) collective-permute-start(f16[4,312,128]{2,1,0:T(8,128)(2,1)S(1)} %pad_maximum_fusion.3), channel_id=1, source_target_pairs={{3,0},{0,1},{1,2},{2,3},{7,4},{4,5},{5,6},{6,7},{11,8},{8,9},{9,10... | collective-permute-start | bytes 958472 | tf_op jit(solution)/shard_map/ppermute | solution.py:726
  142.2 13.1 %copy-start.1 = (f32[16,128,256]{2,1,0:T(8,128)S(1)}, f32[16,128,256]{2,1,0:T(8,128)}, u32[]{:S(2)}) copy-start(f32[16,128,256]{2,1,0:T(8,128)} %get-tuple-element.81.refs_1_) | copy-start | bytes 6291460
  145.3 10.0 %copy-start = (f32[2608,256]{1,0:T(8,128)S(1)}, f32[2608,256]{1,0:T(8,128)}, u32[]{:S(2)}) copy-start(f32[2608,256]{1,0:T(8,128)} %get-tuple-element.79.refs_1_.refs_2_) | copy-start | bytes 8011780
  145.3 10.0 %copy-start.2 = (bf16[16,128,256]{2,1,0:T(8,128)(2,1)S(1)}, bf16[16,128,256]{2,1,0:T(8,128)(2,1)}, u32[]{:S(2)}) copy-start(bf16[16,128,256]{2,1,0:T(8,128)(2,1)} %refs_0_.6) | copy-start | bytes 3145732
  145.3 10.0 %copy-start.5 = (f32[8,256]{1,0:T(8,128)S(1)}, f32[8,256]{1,0:T(8,128)}, u32[]{:S(2)}) copy-start(f32[8,256]{1,0:T(8,128)} %get-tuple-element.80.refs_2_.refs_3_) | copy-start | bytes 24580
  145.3 10.0 %copy-start.7 = (f32[256]{0:T(256)S(1)}, f32[256]{0:T(256)}, u32[]{:S(2)}) copy-start(f32[256]{0:T(256)} %param.10) | copy-start | bytes 3076
  154.0 3.9 %collective-permute-start.19 = (f16[4,312,128]{2,1,0:T(8,128)(2,1)S(1)}, f16[4,312,128]{2,1,0:T(8,128)(2,1)S(1)}, u32[]{:S(2)}, u32[]{:S(2)}) collective-permute-start(f16[4,312,128]{2,1,0:T(8,128)(2,1)S(1)} %pad_maximum_fusion.3), channel_id=1, source_target_pairs={{0,4},{4,0},{8,12},{12,8},{16,20},{20,16},{24,28},{28,24},{1,5},{5... | collective-permute-start | bytes 958472 | tf_op jit(solution)/shard_map/ppermute | solution.py:577
  154.0 3.9 %collective-permute-start.20 = (f16[4,312,128]{2,1,0:T(8,128)(2,1)S(1)}, f16[4,312,128]{2,1,0:T(8,128)(2,1)S(1)}, u32[]{:S(2)}, u32[]{:S(2)}) collective-permute-start(f16[4,312,128]{2,1,0:T(8,128)(2,1)S(1)} %collective-permute-done.16), channel_id=1, source_target_pairs={{0,4},{4,0},{8,12},{12,8},{16,20},{20,16},{24,28},{28,24},{1,5},{5... | collective-permute-start | bytes 958472 | tf_op jit(solution)/shard_map/ppermute | solution.py:577
  154.5 3.5 %collective-permute-start.21 = (f16[4,312,128]{2,1,0:T(8,128)(2,1)S(1)}, f16[4,312,128]{2,1,0:T(8,128)(2,1)S(1)}, u32[]{:S(2)}, u32[]{:S(2)}) collective-permute-start(f16[4,312,128]{2,1,0:T(8,128)(2,1)S(1)} %collective-permute-done.17), channel_id=1, source_target_pairs={{0,4},{4,0},{8,12},{12,8},{16,20},{20,16},{24,28},{28,24},{1,5},{5... | collective-permute-start | bytes 958472 | tf_op jit(solution)/shard_map/ppermute | solution.py:577
  154.5 3.5 %collective-permute-start.22 = (f16[4,312,128]{2,1,0:T(8,128)(2,1)S(1)}, f16[4,312,128]{2,1,0:T(8,128)(2,1)S(1)}, u32[]{:S(2)}, u32[]{:S(2)}) collective-permute-start(f16[4,312,128]{2,1,0:T(8,128)(2,1)S(1)} %collective-permute-done.18), channel_id=1, source_target_pairs={{0,4},{4,0},{8,12},{12,8},{16,20},{20,16},{24,28},{28,24},{1,5},{5... | collective-permute-start | bytes 958472 | tf_op jit(solution)/shard_map/ppermute | solution.py:577

commit v2 on v1

--- a/solution.py
+++ b/solution.py
@@ -393,7 +393,7 @@
             packed[pl.ds(slots[i * 16 + u], 1), :] = value[u : u + 1, :]
         return 0
 
-    lax.fori_loop(0, pull.shape[0] // 16, some, 0, unroll=2)
+    lax.fori_loop(0, pull.shape[0] // 16, some, 0, unroll=4)
 
 
 def flip_weight(weight, flipped):

time: 162 us -> 162 us (level)
  no operation moved by 1% of the time
where the time goes in v2:
time: 162 us; the launch traced here: 161 us
  Pallas kernels  62.1 us (38%)
  starting transfers between devices  44.2 us (27%)
  waiting for transfers between devices  28.8 us (18%)
  local copies, waits for them, and re-layouts  19.8 us (12%)
  other arithmetic  4.63 us (3%)
    pallas_call x13, Pallas kernels, call(): pl.pallas_call(wrapped, in_specs=specs, out_specs=jax.tree.unflatten(jax....  62.1 us
    all_to_all x2, starting transfers between devices, exchange(): return lax.all_to_all(x, AXES, split_axis=0, concat_axis=0, tiled=True)  14.5 us
    gather x1, local copies, waits for them, and re-layouts, body(): quantized = codebook[code_ids]  11.1 us
    ppermute x6, starting transfers between devices, pass_on(): lax.ppermute(x.astype(F16), axis, p)  11.1 us
    ppermute x6, waiting for transfers between devices, pass_on(): lax.ppermute(x.astype(F16), axis, p)  10.5 us
    ppermute x3, waiting for transfers between devices, gather_columns(): lax.ppermute(own, 'col', p)  8.7 us
    ppermute x3, waiting for transfers between devices, gather_rows(): return jnp.stack([own] + [lax.ppermute(own, 'row', p) for p in steps])  6.08 us
    unnamed x38, local copies, waits for them, and re-layouts  5.57 us
  transfers between devices with their start and end apart: 25, of which 8 were waited for; matrix products, arithmetic and copies ran while one was open for 4% of the time, Pallas kernels for 35%

profile of v2, /device:TPU:0, one launch (start us, length us, event | category | flops | bytes accessed | tf_op | source)
XLA Modules:
  0.0 160.8 jit_solution(983030875020155738)
XLA Ops:
  0.6 3.2 %shard_map.135 = (f32[32,8,128]{2,1,0:T(8,128)}, s32[16,128]{1,0:T(8,128)}) custom-call(bf16[16,128,256]{2,1,0:T(8,128)(2,1)} %refs_0_.6, s32[16,128]{1,0:T(8,128)} %refs_1_.1), custom_call_target="tpu_custom_call" | custom-call | flops 1000000000 | bytes 1000000 | tf_op jit(solution)/shard_map/pallas_call | solution.py:61
  3.9 11.1 %gather_fusion = bf16[2048,256]{1,0:T(8,128)(2,1)S(1)} fusion(bf16[16384,256]{1,0:T(8,128)(2,1)} %param.13, s32[2048]{0:T(1024)S(1)} %fusion.3), kind=kCustom, calls=%fused_computation | custom fusion | bytes 2105344 | tf_op jit(solution)/shard_map/gather | solution.py:814
  15.0 0.0 copy-start.11
  15.0 1.3 slice_bitcast_fusion.6
  16.4 0.1 pad_maximum_fusion.5
  16.4 1.3 collective-permute-start.1
  17.7 0.1 pad_maximum_fusion.4
  17.8 5.5 %collective-permute-start = (bf16[3,16,2,256]{3,2,1,0:T(2,128)(2,1)S(1)}, bf16[3,16,2,256]{3,2,1,0:T(2,128)(2,1)S(1)}, u32[]{:S(2)}, u32[]{:S(2)}) collective-permute-start(bf16[3,16,2,256]{3,2,1,0:T(2,128)(2,1)S(1)} %pad_maximum_fusion.4), channel_id=1, source_target_pairs={{0,1},{1,2},{2,3},{4,5},{5,6},{6,7},{8,9},{9,10},{10,11},{12,13},{... | collective-permute-start | bytes 147464 | tf_op jit(solution)/shard_map/ppermute | solution.py:765
  23.3 1.1 slice_bitcast_fusion
  24.5 0.5 collective-permute-done.refs_1_.refs_2_.refs_6_
  25.1 0.1 pad_maximum_fusion.2
  25.2 1.3 collective-permute-start.3
  26.5 0.1 pad_maximum_fusion.1
  26.6 3.1 %collective-permute-start.2 = (bf16[3,2,132,256]{3,2,1,0:T(8,128)(2,1)S(1)}, bf16[3,2,132,256]{3,2,1,0:T(8,128)(2,1)S(1)}, u32[]{:S(2)}, u32[]{:S(2)}) collective-permute-start(bf16[3,2,132,256]{3,2,1,0:T(8,128)(2,1)S(1)} %pad_maximum_fusion.1), channel_id=1, source_target_pairs={{0,4},{4,8},{8,12},{12,16},{16,20},{20,24},{24,28},{1,5},{5,9},{9,... | collective-permute-start | bytes 1216520 | tf_op jit(solution)/shard_map/ppermute | solution.py:771
  29.7 8.3 %all-to-all-start = ((f32[32,8,128]{2,1,0:T(8,128)}), f32[32,8,128]{2,1,0:T(8,128)S(1)}, u32[]{:S(2)}, u32[]{:S(2)}) async-start(f32[32,8,128]{2,1,0:T(8,128)} %get-tuple-element.60), calls=%async_computation | async-start | bytes 262144 | tf_op jit(solution)/shard_map/all_to_all | solution.py:572
  38.0 0.7 copy-done.17
  38.7 0.8 copy-done.18
  39.5 6.7 %shard_map.137 = (f32[2304,128]{1,0:T(8,128)}, f32[2304,128]{1,0:T(8,128)}) custom-call(bf16[16,128,256]{2,1,0:T(8,128)(2,1)} %refs_0_.4, bf16[16,128,256]{2,1,0:T(8,128)(2,1)} %bitcast.54, bf16[3,16,2,256]{3,2,1,0:T(2,128)(2,1)} %copy-done.16, bf16[3,16,2,256]{3,2,1,0:T(2,128)(2,1)} %copy-done.15, bf16[3,2,132,256]{3,2,1,0:T(8,128)(2,1)} %copy-done.18, ...), custom_call_target="tpu_custom_call" | custom-call | flops 2415919104 | bytes 5000000 | tf_op jit(solution)/shard_map/pallas_call | solution.py:61
  46.2 0.1 collective-permute-start.4
  46.4 0.5 copy-done.12
  46.9 10.0 %shard_map.138 = (f32[2608,256]{1,0:T(8,128)}, f32[2048,256]{1,0:T(8,128)}, bf16[256,2304]{1,0:T(8,128)(2,1)}, f32[8,256]{1,0:T(8,128)}, f32[8,256]{1,0:T(8,128)}) custom-call(bf16[16,128,256]{2,1,0:T(8,128)(2,1)} %refs_0_.6, bf16[3,16,2,256]{3,2,1,0:T(2,128)(2,1)} %copy-done.16, bf16[3,16,2,256]{3,2,1,0:T(2,128)(2,1)} %copy-done.15, ...), custom_call_target="tpu_custom_call" | custom-call | flops 2415919104 | bytes 10000000 | tf_op jit(solution)/shard_map/pallas_call | solution.py:61
  56.9 1.6 copy-done.9
  58.5 0.7 copy-done.10
  59.2 5.5 %shard_map.139 = f32[4096,256]{1,0:T(8,128)S(1)} custom-call(s32[2048]{0:T(1024)S(1)} %bitcast.52, f32[2048,256]{1,0:T(8,128)S(1)} %copy-done.9, f32[8,256]{1,0:T(8,128)S(1)} %copy-done.10), custom_call_target="tpu_custom_call" | custom-call | flops 5000000000 | bytes 6000000 | tf_op jit(solution)/shard_map/pallas_call | solution.py:61
  64.7 1.6 convert_element_type.80
  66.3 6.2 %all-to-all-start.1 = ((f16[32,128,256]{2,1,0:T(8,128)(2,1)}), f16[32,128,256]{2,1,0:T(8,128)(2,1)S(1)}, u32[]{:S(2)}, u32[]{:S(2)}) async-start(f16[32,128,256]{2,1,0:T(8,128)(2,1)} %bitcast.19), calls=%async_computation.1 | async-start | bytes 4194304 | tf_op jit(solution)/shard_map/all_to_all | solution.py:572
  72.5 12.8 %shard_map.140 = (f32[2608,256]{1,0:T(8,128)}, f32[2312,128]{1,0:T(8,128)}, f32[2312,128]{1,0:T(8,128)}) custom-call(bf16[16,128,256]{2,1,0:T(8,128)(2,1)} %refs_0_.4, bf16[3,16,2,256]{3,2,1,0:T(2,128)(2,1)} %copy-done.16, bf16[3,16,2,256]{3,2,1,0:T(2,128)(2,1)} %copy-done.15, bf16[3,2,132,256]{3,2,1,0:T(8,128)(2,1)} %copy-done.18, ...), custom_call_target="tpu_custom_call" | custom-call | flops 4831838208 | bytes 15000000 | tf_op jit(solution)/shard_map/pallas_call | solution.py:61
  85.3 0.1 collective-permute-start.5
  85.4 3.0 %collective-permute-done.5.refs_1_ = f32[2312,128]{1,0:T(8,128)S(1)} collective-permute-done((f32[2312,128]{1,0:T(8,128)}, f32[2312,128]{1,0:T(8,128)S(1)}, u32[]{:S(2)}, u32[]{:S(2)}) %collective-permute-start.5) | collective-permute-done | bytes 1183776 | tf_op jit(solution)/shard_map/ppermute | solution.py:577
  88.4 1.3 copy-done.3
  89.7 0.5 shard_map.141
  90.3 2.5 %collective-permute-start.6 = (f16[1168,128]{1,0:T(8,128)(2,1)S(1)}, f16[1168,128]{1,0:T(8,128)(2,1)S(1)}, u32[]{:S(2)}, u32[]{:S(2)}) collective-permute-start(f16[1168,128]{1,0:T(8,128)(2,1)S(1)} %convert_element_type.81), channel_id=1, source_target_pairs={{1,0},{2,1},{3,2},{0,3},{5,4},{6,5},{7,6},{4,7},{9,8},{10,9},{11,1... | collective-permute-start | bytes 897032 | tf_op jit(solution)/shard_map/ppermute | solution.py:684
  92.9 0.6 collective-permute-start.7
  93.5 0.9 collective-permute-start.8
  94.4 6.6 %shard_map.136 = bf16[16,128,256]{2,1,0:T(8,128)(2,1)} custom-call(bf16[16,128,256]{2,1,0:T(8,128)(2,1)} %bitcast.57, bf16[3,16,2,256]{3,2,1,0:T(2,128)(2,1)} %copy-done.16, bf16[3,16,2,256]{3,2,1,0:T(2,128)(2,1)} %copy-done.15, bf16[3,2,132,256]{3,2,1,0:T(8,128)(2,1)} %copy-done.18, bf16[3,2,132,256]{3,2,1,0:T(8,128)(2,1)} %copy-done.17, ...), custom_call_target="tpu_custom_call" | custom-call | flops 2415919104 | bytes 4000000 | tf_op jit(solution)/shard_map/pallas_call | solution.py:61
  101.1 8.4 %shard_map.142 = (f32[16,128,256]{2,1,0:T(8,128)}, f32[8,128]{1,0:T(8,128)}) custom-call(bf16[16,128,256]{2,1,0:T(8,128)(2,1)} %refs_0_.6, f32[2608,256]{1,0:T(8,128)} %get-tuple-element.79.refs_1_.refs_2_, f32[8,256]{1,0:T(8,128)} %get-tuple-element.80.refs_2_.refs_3_, f32[1,256]{1,0:T(1,128)} %bitcast.50, f32[1,256]{1,0:T(1,128)} %bitcast.70, ...), custom_call_target="tpu_custom_call" | custom-call | flops 2415919104 | bytes 8000000 | tf_op jit(solution)/shard_map/pallas_call | solution.py:61
  109.5 0.1 collective-permute-start.12
  109.6 4.9 %collective-permute-done.7 = f16[1168,128]{1,0:T(8,128)(2,1)S(1)} collective-permute-done((f16[1168,128]{1,0:T(8,128)(2,1)S(1)}, f16[1168,128]{1,0:T(8,128)(2,1)S(1)}, u32[]{:S(2)}, u32[]{:S(2)}) %collective-permute-start.7) | collective-permute-done | bytes 299040 | tf_op jit(solution)/shard_map/ppermute | solution.py:684
  114.6 0.4 shard_map.143
  115.1 2.8 %collective-permute-start.9 = (f16[304,128]{1,0:T(8,128)(2,1)S(1)}, f16[304,128]{1,0:T(8,128)(2,1)S(1)}, u32[]{:S(2)}, u32[]{:S(2)}) collective-permute-start(f16[304,128]{1,0:T(8,128)(2,1)S(1)} %convert_element_type.90), channel_id=1, source_target_pairs={{8,0},{12,4},{16,8},{20,12},{24,16},{28,20},{0,24},{4,28},{9,1},{1... | collective-permute-start | bytes 233480 | tf_op jit(solution)/shard_map/ppermute | solution.py:684
  117.9 2.2 %collective-permute-start.10 = (f16[304,128]{1,0:T(8,128)(2,1)S(1)}, f16[304,128]{1,0:T(8,128)(2,1)S(1)}, u32[]{:S(2)}, u32[]{:S(2)}) collective-permute-start(f16[304,128]{1,0:T(8,128)(2,1)S(1)} %convert_element_type.92), channel_id=1, source_target_pairs={{16,0},{20,4},{24,8},{28,12},{0,16},{4,20},{8,24},{12,28},{17,1},{... | collective-permute-start | bytes 233480 | tf_op jit(solution)/shard_map/ppermute | solution.py:684
  120.1 2.1 %collective-permute-start.11 = (f16[304,128]{1,0:T(8,128)(2,1)S(1)}, f16[304,128]{1,0:T(8,128)(2,1)S(1)}, u32[]{:S(2)}, u32[]{:S(2)}) collective-permute-start(f16[304,128]{1,0:T(8,128)(2,1)S(1)} %convert_element_type.94), channel_id=1, source_target_pairs={{24,0},{28,4},{0,8},{4,12},{8,16},{12,20},{16,24},{20,28},{25,1},{... | collective-permute-start | bytes 233480 | tf_op jit(solution)/shard_map/ppermute | solution.py:684
  122.2 5.5 %collective-permute-done.10 = f16[304,128]{1,0:T(8,128)(2,1)S(1)} collective-permute-done((f16[304,128]{1,0:T(8,128)(2,1)S(1)}, f16[304,128]{1,0:T(8,128)(2,1)S(1)}, u32[]{:S(2)}, u32[]{:S(2)}) %collective-permute-start.10) | collective-permute-done | bytes 77856 | tf_op jit(solution)/shard_map/ppermute | solution.py:684
  127.8 0.2 shard_map.144
  128.0 0.6 collective-permute-start.13
  128.6 0.3 collective-permute-start.14
  128.9 1.7 %collective-permute-start.15 = (f16[312,128]{1,0:T(8,128)(2,1)S(1)}, f16[312,128]{1,0:T(8,128)(2,1)S(1)}, u32[]{:S(2)}, u32[]{:S(2)}) collective-permute-start(f16[312,128]{1,0:T(8,128)(2,1)S(1)} %convert_element_type.98), channel_id=1, source_target_pairs={{24,0},{28,4},{0,8},{4,12},{8,16},{12,20},{16,24},{20,28},{25,1},{... | collective-permute-start | bytes 239624 | tf_op jit(solution)/shard_map/ppermute | solution.py:722
  130.6 2.4 %collective-permute-done.13 = f16[312,128]{1,0:T(8,128)(2,1)S(1)} collective-permute-done((f16[312,128]{1,0:T(8,128)(2,1)S(1)}, f16[312,128]{1,0:T(8,128)(2,1)S(1)}, u32[]{:S(2)}, u32[]{:S(2)}) %collective-permute-start.13) | collective-permute-done | bytes 79904 | tf_op jit(solution)/shard_map/ppermute | solution.py:722
  133.0 3.7 %collective-permute-done.14 = f16[312,128]{1,0:T(8,128)(2,1)S(1)} collective-permute-done((f16[312,128]{1,0:T(8,128)(2,1)S(1)}, f16[312,128]{1,0:T(8,128)(2,1)S(1)}, u32[]{:S(2)}, u32[]{:S(2)}) %collective-permute-start.14) | collective-permute-done | bytes 79904 | tf_op jit(solution)/shard_map/ppermute | solution.py:722
  136.7 0.1 pad_maximum_fusion.3
  136.8 2.7 %collective-permute-start.16 = (f16[4,312,128]{2,1,0:T(8,128)(2,1)S(1)}, f16[4,312,128]{2,1,0:T(8,128)(2,1)S(1)}, u32[]{:S(2)}, u32[]{:S(2)}) collective-permute-start(f16[4,312,128]{2,1,0:T(8,128)(2,1)S(1)} %pad_maximum_fusion.3), channel_id=1, source_target_pairs={{1,0},{2,1},{3,2},{0,3},{5,4},{6,5},{7,6},{4,7},{9,8},{10,9},{11,1... | collective-permute-start | bytes 958472 | tf_op jit(solution)/shard_map/ppermute | solution.py:726
  139.6 0.2 collective-permute-start.17
  139.8 0.6 collective-permute-start.18
  140.4 0.6 convert_multiply_fusion
  141.0 0.9 reduce-precision_convert_fusion
  141.9 0.3 pad_maximum_fusion.refs_1_
  142.3 3.1 %shard_map.145 = f32[512,256]{1,0:T(8,128)} custom-call(s32[32,128]{1,0:T(8,128)S(1)} %fusion.1.refs_0_, bf16[4096,512]{1,0:T(8,128)(2,1)S(1)} %pad_maximum_fusion.refs_1_), custom_call_target="tpu_custom_call" | custom-call | flops 2000000000 | bytes 6000000 | tf_op jit(solution)/shard_map/pallas_call | solution.py:61
  145.4 2.2 %collective-permute-done.16 = f16[4,312,128]{2,1,0:T(8,128)(2,1)S(1)} collective-permute-done((f16[4,312,128]{2,1,0:T(8,128)(2,1)S(1)}, f16[4,312,128]{2,1,0:T(8,128)(2,1)S(1)}, u32[]{:S(2)}, u32[]{:S(2)}) %collective-permute-start.16) | collective-permute-done | bytes 319520 | tf_op jit(solution)/shard_map/ppermute | solution.py:726
  147.6 6.5 %collective-permute-done.17 = f16[4,312,128]{2,1,0:T(8,128)(2,1)S(1)} collective-permute-done((f16[4,312,128]{2,1,0:T(8,128)(2,1)S(1)}, f16[4,312,128]{2,1,0:T(8,128)(2,1)S(1)}, u32[]{:S(2)}, u32[]{:S(2)}) %collective-permute-start.17) | collective-permute-done | bytes 319520 | tf_op jit(solution)/shard_map/ppermute | solution.py:726
  154.1 0.5 collective-permute-start.20
  154.6 0.5 collective-permute-start.22
  155.4 2.0 %shard_map.146 = (bf16[16,128,256]{2,1,0:T(8,128)(2,1)}, f32[2,256]{1,0:T(2,128)S(1)}) custom-call(bf16[16,128,256]{2,1,0:T(8,128)(2,1)S(1)} %copy-done.2, f32[16,128,256]{2,1,0:T(8,128)S(1)} %copy-done.1, f32[2608,256]{1,0:T(8,128)S(1)} %copy-done, f32[8,256]{1,0:T(8,128)S(1)} %copy-done.5, f32[1,256]{1,0:T(1,128)S(1)} %bitcast.51, ...), custom_call_target="tpu_custom_call" | custom-call | flops 100000000 | bytes 6000000 | tf_op jit(solution)/shard_map/pallas_call | solution.py:61
  157.4 0.6 fusion.7
  158.2 2.6 %shard_map.147 = (f32[16,144,256]{2,1,0:T(8,128)}, f32[16,144,256]{2,1,0:T(8,128)}) custom-call(f32[4,312,128]{2,1,0:T(8,128)S(1)} %convert_element_type.99.refs_5_.refs_0_, f32[4,312,128]{2,1,0:T(8,128)S(1)} %convert_element_type.100.refs_6_.refs_1_, f32[4,312,128]{2,1,0:T(8,128)S(1)} %convert_element_type.101.refs_7_.refs_2_, ...), custom_call_target="tpu_custom_call" | custom-call | bytes 10000000 | tf_op jit(solution)/shard_map/pallas_call | solution.py:61
  (80 shorter events, 0.9 us)
Async XLA Ops:
  0.6 3.2 %copy-start.14 = (s32[16,128]{1,0:T(8,128)S(1)}, s32[16,128]{1,0:T(8,128)}, u32[]{:S(2)}) copy-start(s32[16,128]{1,0:T(8,128)} %refs_1_.1) | copy-start | bytes 24580
  15.0 23.0 %copy-start.11 = (bf16[2048,256]{1,0:T(8,128)(2,1)}, bf16[2048,256]{1,0:T(8,128)(2,1)S(1)}, u32[]{:S(2)}) copy-start(bf16[2048,256]{1,0:T(8,128)(2,1)S(1)} %gather_fusion) | copy-start | bytes 3145732
  16.4 8.0 %collective-permute-start.1 = (bf16[3,16,2,256]{3,2,1,0:T(2,128)(2,1)S(1)}, bf16[3,16,2,256]{3,2,1,0:T(2,128)(2,1)S(1)}, u32[]{:S(2)}, u32[]{:S(2)}) collective-permute-start(bf16[3,16,2,256]{3,2,1,0:T(2,128)(2,1)S(1)} %pad_maximum_fusion.5), channel_id=1, source_target_pairs={{1,0},{2,1},{3,2},{5,4},{6,5},{7,6},{9,8},{10,9},{11,10},{13,12},{... | collective-permute-start | bytes 147464 | tf_op jit(solution)/shard_map/ppermute | solution.py:766
  17.8 7.2 %collective-permute-start = (bf16[3,16,2,256]{3,2,1,0:T(2,128)(2,1)S(1)}, bf16[3,16,2,256]{3,2,1,0:T(2,128)(2,1)S(1)}, u32[]{:S(2)}, u32[]{:S(2)}) collective-permute-start(bf16[3,16,2,256]{3,2,1,0:T(2,128)(2,1)S(1)} %pad_maximum_fusion.4), channel_id=1, source_target_pairs={{0,1},{1,2},{2,3},{4,5},{5,6},{6,7},{8,9},{9,10},{10,11},{12,13},{... | collective-permute-start | bytes 147464 | tf_op jit(solution)/shard_map/ppermute | solution.py:765
  24.5 13.5 %copy-start.15 = (bf16[3,16,2,256]{3,2,1,0:T(2,128)(2,1)}, bf16[3,16,2,256]{3,2,1,0:T(2,128)(2,1)S(1)}, u32[]{:S(2)}) copy-start(bf16[3,16,2,256]{3,2,1,0:T(2,128)(2,1)S(1)} %collective-permute-done.1.refs_2_.refs_3_.refs_7_) | copy-start | bytes 147460
  25.0 13.0 %copy-start.16 = (bf16[3,16,2,256]{3,2,1,0:T(2,128)(2,1)}, bf16[3,16,2,256]{3,2,1,0:T(2,128)(2,1)S(1)}, u32[]{:S(2)}) copy-start(bf16[3,16,2,256]{3,2,1,0:T(2,128)(2,1)S(1)} %collective-permute-done.refs_1_.refs_2_.refs_6_) | copy-start | bytes 147460
  25.2 12.8 %collective-permute-start.3 = (bf16[3,2,132,256]{3,2,1,0:T(8,128)(2,1)S(1)}, bf16[3,2,132,256]{3,2,1,0:T(8,128)(2,1)S(1)}, u32[]{:S(2)}, u32[]{:S(2)}) collective-permute-start(bf16[3,2,132,256]{3,2,1,0:T(8,128)(2,1)S(1)} %pad_maximum_fusion.2), channel_id=1, source_target_pairs={{4,0},{8,4},{12,8},{16,12},{20,16},{24,20},{28,24},{5,1},{9,5},{13... | collective-permute-start | bytes 1216520 | tf_op jit(solution)/shard_map/ppermute | solution.py:772
  26.6 11.4 %collective-permute-start.2 = (bf16[3,2,132,256]{3,2,1,0:T(8,128)(2,1)S(1)}, bf16[3,2,132,256]{3,2,1,0:T(8,128)(2,1)S(1)}, u32[]{:S(2)}, u32[]{:S(2)}) collective-permute-start(bf16[3,2,132,256]{3,2,1,0:T(8,128)(2,1)S(1)} %pad_maximum_fusion.1), channel_id=1, source_target_pairs={{0,4},{4,8},{8,12},{12,16},{16,20},{20,24},{24,28},{1,5},{5,9},{9,... | collective-permute-start | bytes 1216520 | tf_op jit(solution)/shard_map/ppermute | solution.py:771
  29.7 16.5 %all-to-all-start = ((f32[32,8,128]{2,1,0:T(8,128)}), f32[32,8,128]{2,1,0:T(8,128)S(1)}, u32[]{:S(2)}, u32[]{:S(2)}) async-start(f32[32,8,128]{2,1,0:T(8,128)} %get-tuple-element.60), calls=%async_computation | async-start | bytes 262144 | tf_op jit(solution)/shard_map/all_to_all | solution.py:572
  38.0 0.8 copy-start.17
  38.7 0.8 copy-start.18
  46.2 0.6 copy-start.12
  46.2 20.1 %collective-permute-start.4 = (f32[2304,128]{1,0:T(8,128)}, f32[2304,128]{1,0:T(8,128)S(1)}, u32[]{:S(2)}, u32[]{:S(2)}) collective-permute-start(f32[2304,128]{1,0:T(8,128)} %get-tuple-element.67), channel_id=1, source_target_pairs={{0,4},{4,0},{8,12},{12,8},{16,20},{20,16},{24,28},{28,24},{1,5},{5... | collective-permute-start | bytes 3538952 | tf_op jit(solution)/shard_map/ppermute | solution.py:577
  46.9 10.0 %copy-start.8 = (s32[16,128]{1,0:T(8,128)S(1)}, s32[16,128]{1,0:T(8,128)}, u32[]{:S(2)}) copy-start(s32[16,128]{1,0:T(8,128)} %get-tuple-element.59) | copy-start | bytes 24580
  56.9 1.6 copy-start.9
  58.5 0.7 copy-start.10
  66.3 74.1 %all-to-all-start.1 = ((f16[32,128,256]{2,1,0:T(8,128)(2,1)}), f16[32,128,256]{2,1,0:T(8,128)(2,1)S(1)}, u32[]{:S(2)}, u32[]{:S(2)}) async-start(f16[32,128,256]{2,1,0:T(8,128)(2,1)} %bitcast.19), calls=%async_computation.1 | async-start | bytes 4194304 | tf_op jit(solution)/shard_map/all_to_all | solution.py:572
  72.5 15.9 %copy-start.4 = (f32[2304,128]{1,0:T(8,128)S(1)}, f32[2304,128]{1,0:T(8,128)}, u32[]{:S(2)}) copy-start(f32[2304,128]{1,0:T(8,128)} %get-tuple-element.72.refs_2_) | copy-start | bytes 3538948
  85.3 3.1 %collective-permute-start.5 = (f32[2312,128]{1,0:T(8,128)}, f32[2312,128]{1,0:T(8,128)S(1)}, u32[]{:S(2)}, u32[]{:S(2)}) collective-permute-start(f32[2312,128]{1,0:T(8,128)} %get-tuple-element.71), channel_id=1, source_target_pairs={{0,4},{4,0},{8,12},{12,8},{16,20},{20,16},{24,28},{28,24},{1,5},{5... | collective-permute-start | bytes 3551240 | tf_op jit(solution)/shard_map/ppermute | solution.py:577
  88.4 1.3 copy-start.3
  90.3 19.2 %collective-permute-start.6 = (f16[1168,128]{1,0:T(8,128)(2,1)S(1)}, f16[1168,128]{1,0:T(8,128)(2,1)S(1)}, u32[]{:S(2)}, u32[]{:S(2)}) collective-permute-start(f16[1168,128]{1,0:T(8,128)(2,1)S(1)} %convert_element_type.81), channel_id=1, source_target_pairs={{1,0},{2,1},{3,2},{0,3},{5,4},{6,5},{7,6},{4,7},{9,8},{10,9},{11,1... | collective-permute-start | bytes 897032 | tf_op jit(solution)/shard_map/ppermute | solution.py:684
  92.9 21.7 %collective-permute-start.7 = (f16[1168,128]{1,0:T(8,128)(2,1)S(1)}, f16[1168,128]{1,0:T(8,128)(2,1)S(1)}, u32[]{:S(2)}, u32[]{:S(2)}) collective-permute-start(f16[1168,128]{1,0:T(8,128)(2,1)S(1)} %convert_element_type.83), channel_id=1, source_target_pairs={{2,0},{3,1},{0,2},{1,3},{6,4},{7,5},{4,6},{5,7},{10,8},{11,9},{8,1... | collective-permute-start | bytes 897032 | tf_op jit(solution)/shard_map/ppermute | solution.py:684
  93.5 21.1 %collective-permute-start.8 = (f16[1168,128]{1,0:T(8,128)(2,1)S(1)}, f16[1168,128]{1,0:T(8,128)(2,1)S(1)}, u32[]{:S(2)}, u32[]{:S(2)}) collective-permute-start(f16[1168,128]{1,0:T(8,128)(2,1)S(1)} %convert_element_type.85), channel_id=1, source_target_pairs={{3,0},{0,1},{1,2},{2,3},{7,4},{4,5},{5,6},{6,7},{11,8},{8,9},{9,10... | collective-permute-start | bytes 897032 | tf_op jit(solution)/shard_map/ppermute | solution.py:684
  94.4 6.6 %copy-start.13 = (f32[32,8,128]{2,1,0:T(8,128)S(1)}, f32[32,8,128]{2,1,0:T(8,128)}, u32[]{:S(2)}) copy-start(f32[32,8,128]{2,1,0:T(8,128)} %copy-done.12) | copy-start | bytes 393220
  109.5 18.3 %collective-permute-start.12 = (f32[8,128]{1,0:T(8,128)}, f32[8,128]{1,0:T(8,128)S(1)}, u32[]{:S(2)}, u32[]{:S(2)}) collective-permute-start(f32[8,128]{1,0:T(8,128)} %get-tuple-element.91.refs_4_), channel_id=1, source_target_pairs={{0,4},{4,0},{8,12},{12,8},{16,20},{20,16},{24,28},{28,24},{1,5},{5... | collective-permute-start | bytes 12296 | tf_op jit(solution)/shard_map/ppermute | solution.py:577
  114.6 13.2 %copy-start.6 = (f32[8,128]{1,0:T(8,128)S(1)}, f32[8,128]{1,0:T(8,128)}, u32[]{:S(2)}) copy-start(f32[8,128]{1,0:T(8,128)} %get-tuple-element.91.refs_4_) | copy-start | bytes 12292
  115.1 7.1 %collective-permute-start.9 = (f16[304,128]{1,0:T(8,128)(2,1)S(1)}, f16[304,128]{1,0:T(8,128)(2,1)S(1)}, u32[]{:S(2)}, u32[]{:S(2)}) collective-permute-start(f16[304,128]{1,0:T(8,128)(2,1)S(1)} %convert_element_type.90), channel_id=1, source_target_pairs={{8,0},{12,4},{16,8},{20,12},{24,16},{28,20},{0,24},{4,28},{9,1},{1... | collective-permute-start | bytes 233480 | tf_op jit(solution)/shard_map/ppermute | solution.py:684
  117.9 9.9 %collective-permute-start.10 = (f16[304,128]{1,0:T(8,128)(2,1)S(1)}, f16[304,128]{1,0:T(8,128)(2,1)S(1)}, u32[]{:S(2)}, u32[]{:S(2)}) collective-permute-start(f16[304,128]{1,0:T(8,128)(2,1)S(1)} %convert_element_type.92), channel_id=1, source_target_pairs={{16,0},{20,4},{24,8},{28,12},{0,16},{4,20},{8,24},{12,28},{17,1},{... | collective-permute-start | bytes 233480 | tf_op jit(solution)/shard_map/ppermute | solution.py:684
  120.1 7.7 %collective-permute-start.11 = (f16[304,128]{1,0:T(8,128)(2,1)S(1)}, f16[304,128]{1,0:T(8,128)(2,1)S(1)}, u32[]{:S(2)}, u32[]{:S(2)}) collective-permute-start(f16[304,128]{1,0:T(8,128)(2,1)S(1)} %convert_element_type.94), channel_id=1, source_target_pairs={{24,0},{28,4},{0,8},{4,12},{8,16},{12,20},{16,24},{20,28},{25,1},{... | collective-permute-start | bytes 233480 | tf_op jit(solution)/shard_map/ppermute | solution.py:684
  128.0 5.0 %collective-permute-start.13 = (f16[312,128]{1,0:T(8,128)(2,1)S(1)}, f16[312,128]{1,0:T(8,128)(2,1)S(1)}, u32[]{:S(2)}, u32[]{:S(2)}) collective-permute-start(f16[312,128]{1,0:T(8,128)(2,1)S(1)} %convert_element_type.98), channel_id=1, source_target_pairs={{8,0},{12,4},{16,8},{20,12},{24,16},{28,20},{0,24},{4,28},{9,1},{1... | collective-permute-start | bytes 239624 | tf_op jit(solution)/shard_map/ppermute | solution.py:722
  128.6 8.1 %collective-permute-start.14 = (f16[312,128]{1,0:T(8,128)(2,1)S(1)}, f16[312,128]{1,0:T(8,128)(2,1)S(1)}, u32[]{:S(2)}, u32[]{:S(2)}) collective-permute-start(f16[312,128]{1,0:T(8,128)(2,1)S(1)} %convert_element_type.98), channel_id=1, source_target_pairs={{16,0},{20,4},{24,8},{28,12},{0,16},{4,20},{8,24},{12,28},{17,1},{... | collective-permute-start | bytes 239624 | tf_op jit(solution)/shard_map/ppermute | solution.py:722
  128.9 7.8 %collective-permute-start.15 = (f16[312,128]{1,0:T(8,128)(2,1)S(1)}, f16[312,128]{1,0:T(8,128)(2,1)S(1)}, u32[]{:S(2)}, u32[]{:S(2)}) collective-permute-start(f16[312,128]{1,0:T(8,128)(2,1)S(1)} %convert_element_type.98), channel_id=1, source_target_pairs={{24,0},{28,4},{0,8},{4,12},{8,16},{12,20},{16,24},{20,28},{25,1},{... | collective-permute-start | bytes 239624 | tf_op jit(solution)/shard_map/ppermute | solution.py:722
  136.8 10.7 %collective-permute-start.16 = (f16[4,312,128]{2,1,0:T(8,128)(2,1)S(1)}, f16[4,312,128]{2,1,0:T(8,128)(2,1)S(1)}, u32[]{:S(2)}, u32[]{:S(2)}) collective-permute-start(f16[4,312,128]{2,1,0:T(8,128)(2,1)S(1)} %pad_maximum_fusion.3), channel_id=1, source_target_pairs={{1,0},{2,1},{3,2},{0,3},{5,4},{6,5},{7,6},{4,7},{9,8},{10,9},{11,1... | collective-permute-start | bytes 958472 | tf_op jit(solution)/shard_map/ppermute | solution.py:726
  139.6 14.5 %collective-permute-start.17 = (f16[4,312,128]{2,1,0:T(8,128)(2,1)S(1)}, f16[4,312,128]{2,1,0:T(8,128)(2,1)S(1)}, u32[]{:S(2)}, u32[]{:S(2)}) collective-permute-start(f16[4,312,128]{2,1,0:T(8,128)(2,1)S(1)} %pad_maximum_fusion.3), channel_id=1, source_target_pairs={{2,0},{3,1},{0,2},{1,3},{6,4},{7,5},{4,6},{5,7},{10,8},{11,9},{8,1... | collective-permute-start | bytes 958472 | tf_op jit(solution)/shard_map/ppermute | solution.py:726
  139.8 14.3 %collective-permute-start.18 = (f16[4,312,128]{2,1,0:T(8,128)(2,1)S(1)}, f16[4,312,128]{2,1,0:T(8,128)(2,1)S(1)}, u32[]{:S(2)}, u32[]{:S(2)}) collective-permute-start(f16[4,312,128]{2,1,0:T(8,128)(2,1)S(1)} %pad_maximum_fusion.3), channel_id=1, source_target_pairs={{3,0},{0,1},{1,2},{2,3},{7,4},{4,5},{5,6},{6,7},{11,8},{8,9},{9,10... | collective-permute-start | bytes 958472 | tf_op jit(solution)/shard_map/ppermute | solution.py:726
  142.2 13.1 %copy-start.1 = (f32[16,128,256]{2,1,0:T(8,128)S(1)}, f32[16,128,256]{2,1,0:T(8,128)}, u32[]{:S(2)}) copy-start(f32[16,128,256]{2,1,0:T(8,128)} %get-tuple-element.81.refs_1_) | copy-start | bytes 6291460
  145.4 10.0 %copy-start = (f32[2608,256]{1,0:T(8,128)S(1)}, f32[2608,256]{1,0:T(8,128)}, u32[]{:S(2)}) copy-start(f32[2608,256]{1,0:T(8,128)} %get-tuple-element.79.refs_1_.refs_2_) | copy-start | bytes 8011780
  145.4 10.0 %copy-start.2 = (bf16[16,128,256]{2,1,0:T(8,128)(2,1)S(1)}, bf16[16,128,256]{2,1,0:T(8,128)(2,1)}, u32[]{:S(2)}) copy-start(bf16[16,128,256]{2,1,0:T(8,128)(2,1)} %refs_0_.6) | copy-start | bytes 3145732
  145.4 10.0 %copy-start.5 = (f32[8,256]{1,0:T(8,128)S(1)}, f32[8,256]{1,0:T(8,128)}, u32[]{:S(2)}) copy-start(f32[8,256]{1,0:T(8,128)} %get-tuple-element.80.refs_2_.refs_3_) | copy-start | bytes 24580
  145.4 10.0 %copy-start.7 = (f32[256]{0:T(256)S(1)}, f32[256]{0:T(256)}, u32[]{:S(2)}) copy-start(f32[256]{0:T(256)} %param.10) | copy-start | bytes 3076
  154.1 3.9 %collective-permute-start.19 = (f16[4,312,128]{2,1,0:T(8,128)(2,1)S(1)}, f16[4,312,128]{2,1,0:T(8,128)(2,1)S(1)}, u32[]{:S(2)}, u32[]{:S(2)}) collective-permute-start(f16[4,312,128]{2,1,0:T(8,128)(2,1)S(1)} %pad_maximum_fusion.3), channel_id=1, source_target_pairs={{0,4},{4,0},{8,12},{12,8},{16,20},{20,16},{24,28},{28,24},{1,5},{5... | collective-permute-start | bytes 958472 | tf_op jit(solution)/shard_map/ppermute | solution.py:577
  154.1 3.9 %collective-permute-start.20 = (f16[4,312,128]{2,1,0:T(8,128)(2,1)S(1)}, f16[4,312,128]{2,1,0:T(8,128)(2,1)S(1)}, u32[]{:S(2)}, u32[]{:S(2)}) collective-permute-start(f16[4,312,128]{2,1,0:T(8,128)(2,1)S(1)} %collective-permute-done.16), channel_id=1, source_target_pairs={{0,4},{4,0},{8,12},{12,8},{16,20},{20,16},{24,28},{28,24},{1,5},{5... | collective-permute-start | bytes 958472 | tf_op jit(solution)/shard_map/ppermute | solution.py:577
  154.6 3.5 %collective-permute-start.21 = (f16[4,312,128]{2,1,0:T(8,128)(2,1)S(1)}, f16[4,312,128]{2,1,0:T(8,128)(2,1)S(1)}, u32[]{:S(2)}, u32[]{:S(2)}) collective-permute-start(f16[4,312,128]{2,1,0:T(8,128)(2,1)S(1)} %collective-permute-done.17), channel_id=1, source_target_pairs={{0,4},{4,0},{8,12},{12,8},{16,20},{20,16},{24,28},{28,24},{1,5},{5... | collective-permute-start | bytes 958472 | tf_op jit(solution)/shard_map/ppermute | solution.py:577
  154.6 3.5 %collective-permute-start.22 = (f16[4,312,128]{2,1,0:T(8,128)(2,1)S(1)}, f16[4,312,128]{2,1,0:T(8,128)(2,1)S(1)}, u32[]{:S(2)}, u32[]{:S(2)}) collective-permute-start(f16[4,312,128]{2,1,0:T(8,128)(2,1)S(1)} %collective-permute-done.18), channel_id=1, source_target_pairs={{0,4},{4,0},{8,12},{12,8},{16,20},{20,16},{24,28},{28,24},{1,5},{5... | collective-permute-start | bytes 958472 | tf_op jit(solution)/shard_map/ppermute | solution.py:577
